TPU v7x, 256 devices: a whole 4x4x8 slice. The times are simulated.
256 devices in a mesh: layer: 64 (over z, y_lo, x), strip: 4 (over y_hi, core).
Axes of the slice: x: 4, y: 4 (y_hi: 2, y_lo: 2; y = y_hi * 2 + y_lo), z: 8, core: 2. Of those that a mesh axis runs over, the one named last changes fastest.
Arguments:
- probes: float32 [16, 2, 128, 16384], P(None, None, 'layer', 'strip'), may hold values from -6 to 6
- slowness: float32 [128, 16384], P('layer', 'strip'), may hold values from 0.05 to 0.5
- absorbing: int32 [128], P('layer'), may hold values 0 or 1
- partition: int32 [16384], replicated, may hold values from 0 to 16383, each once
Outputs:
- field: float32 [16, 2, 128, 16384], P(None, None, 'layer', 'strip')
- bases: float32 [256, 2, 32, 64], P(('layer', 'strip'))
Inputs may be any that keep to these rules, and one draw needn't show every extreme that they name: `partition`: each interface point appears exactly once.
All inputs are finite; a program needn't handle non-finite values. No bound on the sum of `absorbing` on one device may be relied on, other than what follows from the above.
Results may differ from a plain program's by a relative error of at most 0.00013.
Values sent between devices are 32-bit elements; how exact they have to be, the bound alone decides.
A program may use at most 128 MiB of HBM per device.

v0:
```python
import jax
import jax.numpy as jnp
from jax import lax
from jax.sharding import PartitionSpec as P

ITERS = 9
BS = 64


OMEGA = 0.8
BETA = 0.5
SIGMA = 1.5


def extended(shard, sides, width):
    for axis, dim in sides:
        peers, length = (lax.axis_size(axis), shard.shape[dim])
        up = [(i, (i + 1) % peers) for i in range(peers - 1)]
        down = [(j, i) for i, j in up]
        last = lax.slice_in_dim(shard, length - width, length, axis=dim)
        leading = lax.slice_in_dim(shard, 0, width, axis=dim)
        before = lax.ppermute(last, axis, up)
        after = lax.ppermute(leading, axis, down)
        shard = jnp.concatenate([before, shard, after], axis=dim)
    return shard


def from_root(value, axis, source):
    kept = jnp.where(lax.axis_index(axis) == source, value, 0).astype(value.dtype)
    return lax.psum(kept, axis)


def coefficients(slowness, absorbing):
    flags = absorbing.astype(jnp.float32)[:, None]
    dre = 4.0 - slowness
    dim = BETA * slowness + SIGMA * flags
    mag = dre * dre + dim * dim
    return (dre, dim, dre / mag, -dim / mag)


def relax(upad, source, dre, dim, ire, iim):
    nbr = upad[..., :-2, 1:-1] + upad[..., 2:, 1:-1] + upad[..., 1:-1, :-2] + upad[..., 1:-1, 2:]
    ure = upad[..., 0, 1:-1, 1:-1]
    uim = upad[..., 1, 1:-1, 1:-1]
    rre = source[..., 0, :, :] - (dre * ure - dim * uim) + nbr[..., 0, :, :]
    rim = source[..., 1, :, :] - (dre * uim + dim * ure) + nbr[..., 1, :, :]
    new_re = ure + OMEGA * (ire * rre - iim * rim)
    new_im = uim + OMEGA * (ire * rim + iim * rre)
    return jnp.stack([new_re, new_im], axis=-3)


def compress(samples):
    gram = jnp.einsum("bmpk,bmqk->bmpq", samples, samples, precision=lax.Precision.HIGHEST)
    lower_factor = jnp.linalg.cholesky(gram)
    return jax.scipy.linalg.solve_triangular(lower_factor, samples, lower=True)


def pick_blocks(traces, index_table, probe_count):
    picked = jnp.take(traces, index_table, axis=3)
    count = index_table.shape[0]
    return jnp.transpose(picked, (3, 0, 1, 2, 4)).reshape(count, 2, 2 * probe_count, BS)


def per_device(probes, slowness, absorbing, partition):
    nlayer = lax.axis_size("layer")
    nstrip = lax.axis_size("strip")
    probe_count = probes.shape[0]
    dre, dim, ire, iim = coefficients(slowness, absorbing)
    field_now = jnp.stack(
        [
            OMEGA * (ire * probes[:, 0] - iim * probes[:, 1]),
            OMEGA * (ire * probes[:, 1] + iim * probes[:, 0]),
        ],
        axis=1,
    )
    for step in range(ITERS - 1):
        padded = extended(field_now, (("layer", 2), ("strip", 3)), 1)
        field_now = relax(padded, probes, dre, dim, ire, iim)
    bottom_row = field_now[:, :, -1, :]
    top_row = field_now[:, :, 0, :]
    total_points = bottom_row.shape[-1] * nstrip
    blocks_here = total_points // (BS * nlayer * nstrip)
    bottom_all, top_all = (
        lax.all_gather(bottom_row, "strip", axis=2, tiled=True),
        lax.all_gather(top_row, "strip", axis=2, tiled=True),
    )
    upper = from_root(bottom_all, "layer", nlayer // 2 - 1)
    lower = from_root(top_all, "layer", nlayer // 2)
    traces = jnp.stack([upper, lower])
    owner = lax.axis_index("layer") * nstrip + lax.axis_index("strip")
    chosen = lax.dynamic_slice_in_dim(partition, owner * (blocks_here * BS), blocks_here * BS)
    index_table = chosen.reshape(blocks_here, BS)
    return (field_now, compress(pick_blocks(traces, index_table, probe_count)))


def solution(mesh):
    return jax.shard_map(
        per_device,
        mesh=mesh,
        in_specs=(P(None, None, "layer", "strip"), P("layer", "strip"), P("layer"), P()),
        out_specs=(P(None, None, "layer", "strip"), P(("layer", "strip"), None, None, None)),
        check_vma=False,
    )
```

profile of v0, /device:TPU:16, one launch (start us, length us, event | category | flops | bytes accessed | tf_op | source)
XLA Modules:
  0.0 1031.2 jit_solution(2771041862917474272)
XLA Ops:
  11.6 3.4 collective-permute-start
  16.3 9.8 collective-permute-done
  26.1 4.1 collective-permute-done.1
  30.4 1.9 collective-permute-start.2
  32.3 5.1 collective-permute-start.3
  37.5 1.9 collective-permute-done.3
  40.9 3.4 collective-permute-start.4
  45.6 6.3 collective-permute-done.4
  51.9 4.1 collective-permute-done.5
  56.1 1.9 collective-permute-start.6
  58.0 5.6 collective-permute-start.7
  67.0 4.4 collective-permute-start.8
  72.7 6.1 collective-permute-done.8
  78.8 4.1 collective-permute-done.9
  83.1 1.9 collective-permute-start.10
  85.0 6.2 collective-permute-start.11
  94.6 4.0 collective-permute-start.12
  100.0 5.5 collective-permute-done.12
  105.5 4.3 collective-permute-done.13
  109.8 1.9 collective-permute-start.14
  111.7 6.7 collective-permute-start.15
  121.9 4.0 collective-permute-start.16
  127.2 5.3 collective-permute-done.16
  132.5 4.4 collective-permute-done.17
  137.0 1.9 collective-permute-start.18
  139.0 6.7 collective-permute-start.19
  149.1 4.2 collective-permute-start.20
  154.6 5.3 collective-permute-done.20
  160.0 4.4 collective-permute-done.21
  164.5 1.9 collective-permute-start.22
  166.4 6.9 collective-permute-start.23
  176.6 5.1 collective-permute-start.24
  182.9 5.3 collective-permute-done.24
  188.3 4.4 collective-permute-done.25
  192.8 1.9 collective-permute-start.26
  194.7 6.7 collective-permute-start.27
  204.8 4.9 collective-permute-start.28
  211.1 5.3 collective-permute-done.28
  216.4 4.4 collective-permute-done.29
  220.9 1.9 collective-permute-start.30
  222.8 6.7 collective-permute-start.31
  234.8 79.7 %all-gather.7.cloned.1.call-done = f32[16,2,1,16384]{3,0,2,1:T(8,128)} async-done(((f32[16,2,1,4096]{3,0,2,1:T(8,128)}), f32[16,2,1,16384]{3,0,2,1:T(8,128)}) %all-gather.7.cloned.1.call-update) | async-done | bytes 2097168 | tf_op jit(solution)/shard_map/all_gather | solution.py:85
  315.9 29.6 %all-gather.5.cloned.1.call-done = f32[16,2,1,16384]{3,0,2,1:T(8,128)} async-done(((f32[16,2,1,4096]{3,0,2,1:T(8,128)}), f32[16,2,1,16384]{3,0,2,1:T(8,128)}) %all-gather.5.cloned.1.call-update) | async-done | bytes 2097168 | tf_op jit(solution)/shard_map/all_gather | solution.py:84
  349.7 620.2 %all-reduce.3.cloned.1.call-done = (f32[1,16,2,16384]{3,1,2,0:T(8,128)}, f32[1,16,2,16384]{3,1,2,0:T(8,128)}) async-done(((f32[1,16,2,16384]{3,1,2,0:T(8,128)}, f32[1,16,2,16384]{3,1,2,0:T(8,128)}), (f32[1,16,2,16384]{3,1,2,0:T(8,128)}, f32[1,16,2,16384]{3,1,2,0:T(8,128)})) %all-reduce.3.cloned.1.call-update) | async-done | bytes 4194320 | tf_op jit(solution)/shard_map/psum | solution.py:30
  970.0 4.6 pad_maximum_fusion
  974.6 36.2 %copy.301 = f32[2,16,2,16384]{1,2,3,0:T(2,128)} copy(f32[2,16,2,16384]{3,1,2,0:T(8,128)} %pad_maximum_fusion) | data formatting | bytes 8388608 | tf_op jit(solution)/shard_map/stack | solution.py:89
  1012.7 5.9 custom-call.8
  1018.8 4.9 custom-call.9
  (84 shorter events, 51.1 us)
Async XLA Ops:
  7.2 307.3 %all-gather.7.cloned.1.call-start = ((), (), s32[]{:S(2)}) async-start(), calls=%async_computation.1 | async-start | bytes 2621440 | tf_op jit(solution)/shard_map/all_gather | solution.py:85
  11.6 14.6 %collective-permute-start = (f32[16,2,1,4096]{3,0,2,1:T(8,128)S(1)}, f32[16,2,1,4096]{3,0,2,1:T(8,128)S(1)}, u32[]{:S(2)}, u32[]{:S(2)}) collective-permute-start(f32[16,2,1,4096]{3,0,2,1:T(8,128)S(1)} %get-tuple-element.66), channel_id=1, source_target_pairs={{0,4},{4,8},{8,12},{12,16},{16,20},{20,24},{24,28},{28,32},{32,36}... | collective-permute-start | bytes 1572872 | tf_op jit(solution)/shard_map/ppermute | solution.py:22
  15.0 15.3 %collective-permute-start.1 = (f32[16,2,1,4096]{3,0,2,1:T(8,128)S(1)}, f32[16,2,1,4096]{3,0,2,1:T(8,128)S(1)}, u32[]{:S(2)}, u32[]{:S(2)}) collective-permute-start(f32[16,2,1,4096]{3,0,2,1:T(8,128)S(1)} %get-tuple-element.67), channel_id=1, source_target_pairs={{4,0},{8,4},{12,8},{16,12},{20,16},{24,20},{28,24},{32,28},{36,32}... | collective-permute-start | bytes 1572872 | tf_op jit(solution)/shard_map/ppermute | solution.py:23
  30.4 7.1 collective-permute-start.2
  32.3 7.0 collective-permute-start.3
  40.9 11.0 %collective-permute-start.4 = (f32[16,2,1,4096]{3,0,2,1:T(8,128)S(1)}, f32[16,2,1,4096]{3,0,2,1:T(8,128)S(1)}, u32[]{:S(2)}, u32[]{:S(2)}) collective-permute-start(f32[16,2,1,4096]{3,0,2,1:T(8,128)S(1)} %get-tuple-element.64), channel_id=1, source_target_pairs={{0,4},{4,8},{8,12},{12,16},{16,20},{20,24},{24,28},{28,32},{32,36}... | collective-permute-start | bytes 1572872 | tf_op jit(solution)/shard_map/ppermute | solution.py:22
  44.3 11.7 %collective-permute-start.5 = (f32[16,2,1,4096]{3,0,2,1:T(8,128)S(1)}, f32[16,2,1,4096]{3,0,2,1:T(8,128)S(1)}, u32[]{:S(2)}, u32[]{:S(2)}) collective-permute-start(f32[16,2,1,4096]{3,0,2,1:T(8,128)S(1)} %get-tuple-element.65), channel_id=1, source_target_pairs={{4,0},{8,4},{12,8},{16,12},{20,16},{24,20},{28,24},{32,28},{36,32}... | collective-permute-start | bytes 1572872 | tf_op jit(solution)/shard_map/ppermute | solution.py:23
  56.1 7.5 collective-permute-start.6
  58.0 7.5 collective-permute-start.7
  67.0 11.8 %collective-permute-start.8 = (f32[16,2,1,4096]{3,0,2,1:T(8,128)S(1)}, f32[16,2,1,4096]{3,0,2,1:T(8,128)S(1)}, u32[]{:S(2)}, u32[]{:S(2)}) collective-permute-start(f32[16,2,1,4096]{3,0,2,1:T(8,128)S(1)} %get-tuple-element.62), channel_id=1, source_target_pairs={{0,4},{4,8},{8,12},{12,16},{16,20},{20,24},{24,28},{28,32},{32,36}... | collective-permute-start | bytes 1572872 | tf_op jit(solution)/shard_map/ppermute | solution.py:22
  71.4 11.6 %collective-permute-start.9 = (f32[16,2,1,4096]{3,0,2,1:T(8,128)S(1)}, f32[16,2,1,4096]{3,0,2,1:T(8,128)S(1)}, u32[]{:S(2)}, u32[]{:S(2)}) collective-permute-start(f32[16,2,1,4096]{3,0,2,1:T(8,128)S(1)} %get-tuple-element.63), channel_id=1, source_target_pairs={{4,0},{8,4},{12,8},{16,12},{20,16},{24,20},{28,24},{32,28},{36,32}... | collective-permute-start | bytes 1572872 | tf_op jit(solution)/shard_map/ppermute | solution.py:23
  83.1 8.1 collective-permute-start.10
  85.0 8.1 collective-permute-start.11
  94.6 10.8 %collective-permute-start.12 = (f32[16,2,1,4096]{3,0,2,1:T(8,128)S(1)}, f32[16,2,1,4096]{3,0,2,1:T(8,128)S(1)}, u32[]{:S(2)}, u32[]{:S(2)}) collective-permute-start(f32[16,2,1,4096]{3,0,2,1:T(8,128)S(1)} %get-tuple-element.60), channel_id=1, source_target_pairs={{0,4},{4,8},{8,12},{12,16},{16,20},{20,24},{24,28},{28,32},{32,36}... | collective-permute-start | bytes 1572872 | tf_op jit(solution)/shard_map/ppermute | solution.py:22
  98.7 11.1 %collective-permute-start.13 = (f32[16,2,1,4096]{3,0,2,1:T(8,128)S(1)}, f32[16,2,1,4096]{3,0,2,1:T(8,128)S(1)}, u32[]{:S(2)}, u32[]{:S(2)}) collective-permute-start(f32[16,2,1,4096]{3,0,2,1:T(8,128)S(1)} %get-tuple-element.61), channel_id=1, source_target_pairs={{4,0},{8,4},{12,8},{16,12},{20,16},{24,20},{28,24},{32,28},{36,32}... | collective-permute-start | bytes 1572872 | tf_op jit(solution)/shard_map/ppermute | solution.py:23
  109.8 8.6 collective-permute-start.14
  111.7 8.6 collective-permute-start.15
  121.9 10.7 %collective-permute-start.16 = (f32[16,2,1,4096]{3,0,2,1:T(8,128)S(1)}, f32[16,2,1,4096]{3,0,2,1:T(8,128)S(1)}, u32[]{:S(2)}, u32[]{:S(2)}) collective-permute-start(f32[16,2,1,4096]{3,0,2,1:T(8,128)S(1)} %get-tuple-element.58), channel_id=1, source_target_pairs={{0,4},{4,8},{8,12},{12,16},{16,20},{20,24},{24,28},{28,32},{32,36}... | collective-permute-start | bytes 1572872 | tf_op jit(solution)/shard_map/ppermute | solution.py:22
  125.9 11.1 %collective-permute-start.17 = (f32[16,2,1,4096]{3,0,2,1:T(8,128)S(1)}, f32[16,2,1,4096]{3,0,2,1:T(8,128)S(1)}, u32[]{:S(2)}, u32[]{:S(2)}) collective-permute-start(f32[16,2,1,4096]{3,0,2,1:T(8,128)S(1)} %get-tuple-element.59), channel_id=1, source_target_pairs={{4,0},{8,4},{12,8},{16,12},{20,16},{24,20},{28,24},{32,28},{36,32}... | collective-permute-start | bytes 1572872 | tf_op jit(solution)/shard_map/ppermute | solution.py:23
  137.0 8.6 collective-permute-start.18
  139.0 8.6 collective-permute-start.19
  149.1 10.9 %collective-permute-start.20 = (f32[16,2,1,4096]{3,0,2,1:T(8,128)S(1)}, f32[16,2,1,4096]{3,0,2,1:T(8,128)S(1)}, u32[]{:S(2)}, u32[]{:S(2)}) collective-permute-start(f32[16,2,1,4096]{3,0,2,1:T(8,128)S(1)} %get-tuple-element.56), channel_id=1, source_target_pairs={{0,4},{4,8},{8,12},{12,16},{16,20},{20,24},{24,28},{28,32},{32,36}... | collective-permute-start | bytes 1572872 | tf_op jit(solution)/shard_map/ppermute | solution.py:22
  153.3 11.1 %collective-permute-start.21 = (f32[16,2,1,4096]{3,0,2,1:T(8,128)S(1)}, f32[16,2,1,4096]{3,0,2,1:T(8,128)S(1)}, u32[]{:S(2)}, u32[]{:S(2)}) collective-permute-start(f32[16,2,1,4096]{3,0,2,1:T(8,128)S(1)} %get-tuple-element.57), channel_id=1, source_target_pairs={{4,0},{8,4},{12,8},{16,12},{20,16},{24,20},{28,24},{32,28},{36,32}... | collective-permute-start | bytes 1572872 | tf_op jit(solution)/shard_map/ppermute | solution.py:23
  164.5 8.8 collective-permute-start.22
  166.4 8.6 collective-permute-start.23
  176.6 11.7 %collective-permute-start.24 = (f32[16,2,1,4096]{3,0,2,1:T(8,128)S(1)}, f32[16,2,1,4096]{3,0,2,1:T(8,128)S(1)}, u32[]{:S(2)}, u32[]{:S(2)}) collective-permute-start(f32[16,2,1,4096]{3,0,2,1:T(8,128)S(1)} %get-tuple-element.54), channel_id=1, source_target_pairs={{0,4},{4,8},{8,12},{12,16},{16,20},{20,24},{24,28},{28,32},{32,36}... | collective-permute-start | bytes 1572872 | tf_op jit(solution)/shard_map/ppermute | solution.py:22
  181.6 11.1 %collective-permute-start.25 = (f32[16,2,1,4096]{3,0,2,1:T(8,128)S(1)}, f32[16,2,1,4096]{3,0,2,1:T(8,128)S(1)}, u32[]{:S(2)}, u32[]{:S(2)}) collective-permute-start(f32[16,2,1,4096]{3,0,2,1:T(8,128)S(1)} %get-tuple-element.55), channel_id=1, source_target_pairs={{4,0},{8,4},{12,8},{16,12},{20,16},{24,20},{28,24},{32,28},{36,32}... | collective-permute-start | bytes 1572872 | tf_op jit(solution)/shard_map/ppermute | solution.py:23
  192.8 8.6 collective-permute-start.26
  194.7 8.6 collective-permute-start.27
  204.8 11.6 %collective-permute-start.28 = (f32[16,2,1,4096]{3,0,2,1:T(8,128)S(1)}, f32[16,2,1,4096]{3,0,2,1:T(8,128)S(1)}, u32[]{:S(2)}, u32[]{:S(2)}) collective-permute-start(f32[16,2,1,4096]{3,0,2,1:T(8,128)S(1)} %get-tuple-element.52), channel_id=1, source_target_pairs={{0,4},{4,8},{8,12},{12,16},{16,20},{20,24},{24,28},{28,32},{32,36}... | collective-permute-start | bytes 1572872 | tf_op jit(solution)/shard_map/ppermute | solution.py:22
  209.8 11.1 %collective-permute-start.29 = (f32[16,2,1,4096]{3,0,2,1:T(8,128)S(1)}, f32[16,2,1,4096]{3,0,2,1:T(8,128)S(1)}, u32[]{:S(2)}, u32[]{:S(2)}) collective-permute-start(f32[16,2,1,4096]{3,0,2,1:T(8,128)S(1)} %get-tuple-element.53), channel_id=1, source_target_pairs={{4,0},{8,4},{12,8},{16,12},{20,16},{24,20},{28,24},{32,28},{36,32}... | collective-permute-start | bytes 1572872 | tf_op jit(solution)/shard_map/ppermute | solution.py:23
  220.9 8.6 collective-permute-start.30
  222.8 8.6 collective-permute-start.31
  234.0 111.5 %all-gather.5.cloned.1.call-start = ((), (), s32[]{:S(2)}) async-start(), calls=%async_computation | async-start | bytes 2621440 | tf_op jit(solution)/shard_map/all_gather | solution.py:84
  234.7 735.2 %all-reduce.3.cloned.1.call-start = ((), (), s32[]{:S(2)}) async-start(), calls=%async_computation.2 | async-start | bytes 8388608 | tf_op jit(solution)/shard_map/psum | solution.py:30
Sparse Core Ops, SparseCore 0:
  234.1 80.3 all-gather.6
  316.8 28.6 all-gather.4
  348.2 621.7 all-reduce.2
where the time goes:
time: 1030 us
  waiting for transfers between devices  829 us (80%)
  starting transfers between devices  110 us (11%)
  local copies, waits for them, and re-layouts  41 us (4%)
  other arithmetic  36.5 us (4%)
  between operations  14.3 us (1%)
    psum x1, waiting for transfers between devices, from_root(): return lax.psum(kept, axis)  620 us
    all_gather x1, waiting for transfers between devices, per_device(): lax.all_gather(top_row, 'strip', axis=2, tiled=True)  79.7 us
    ppermute x16, starting transfers between devices, extended(): after = lax.ppermute(leading, axis, down)  60.8 us
    ppermute x16, waiting for transfers between devices, extended(): after = lax.ppermute(leading, axis, down)  49.2 us
    ppermute x16, waiting for transfers between devices, extended(): before = lax.ppermute(last, axis, up)  49.2 us
    ppermute x16, starting transfers between devices, extended(): before = lax.ppermute(last, axis, up)  48.8 us
    another operation x1, local copies, waits for them, and re-layouts, per_device(): traces = jnp.stack([upper, lower])  36.2 us
    all_gather x1, waiting for transfers between devices, per_device(): lax.all_gather(bottom_row, 'strip', axis=2, tiled=True)  29.6 us
  transfers between devices with their start and end apart: 35, of which 27 were waited for; matrix products, arithmetic and copies ran while one was open for 0% of the time, Pallas kernels for 0%

commit v1 on v0

v1 whole, which is shorter than its diff:
```python
import functools

import jax
import jax.numpy as jnp
from jax import lax
from jax.experimental import pallas as pl
from jax.experimental.pallas import tpu as pltpu
from jax.sharding import PartitionSpec as P

ITERS = 9
BS = 64
OMEGA = 0.8
BETA = 0.5
SIGMA = 1.5

MESH = pl.DeviceIdType.MESH
PLANE = 32
GROUP = 8
PROBES = 16
PAIR = 2
OWN = 2 * GROUP
HALO = 8
ROWS = OWN + 2 * HALO
MAIN = 4
WIDE = 5
F32 = jnp.float32


def lanes():
    return lax.broadcasted_iota(jnp.int32, (8, 128), 1)


def sublanes():
    return lax.broadcasted_iota(jnp.int32, (8, 128), 0)


def widen(tiles, left, right):
    low = lanes() < 64
    sub = sublanes()
    turned = [pltpu.roll(t, 64, 1) for t in tiles]
    left, right = pltpu.roll(left, 64, 1), pltpu.roll(right, 64, 1)
    before = jnp.where(sub == 0, left, pltpu.roll(turned[3], 1, 0))
    after = jnp.where(sub == 7, right, pltpu.roll(turned[0], 7, 0))
    ends = [before] + turned + [after]
    return [jnp.where(low, ends[t], ends[t + 1]) for t in range(WIDE)]


def narrow(wide):
    low = lanes() < 64
    turned = [pltpu.roll(t, 64, 1) for t in wide]
    return [jnp.where(low, turned[t], turned[t + 1]) for t in range(MAIN)]


def beside(row):
    lane = lanes()
    ahead = [pltpu.roll(t, 1, 1) for t in row]
    back = [pltpu.roll(t, 127, 1) for t in row]
    out = []
    for t in range(WIDE):
        left = jnp.where(lane == 0, ahead[t - 1], ahead[t]) if t else ahead[t]
        right = jnp.where(lane == 127, back[t + 1], back[t]) if t < WIDE - 1 else back[t]
        out.append(left + right)
    return out


def kernel(
    probes, slow, absorb, partition,
    field, bases,
    inbuf, slowbuf, flags, esend, erecv, sendf, ssend, fbuf, sbuf, coef, gbuf, ubuf, obuf, rbuf, outbuf,
    points, tbuf, picked, gat, mats, based,
    in_sem, es, er, own_sem, fs, fr, zs, zr, rs, rr, out_sem,
    ts, tr, town, gs, gr, gown, base_sem,
):
    layer = lax.axis_index("layer")
    strip = lax.axis_index("strip")
    z = layer // GROUP
    me = lax.rem(layer, GROUP)

    def peer_of(j):
        return lax.rem(me + j, GROUP)

    def from_of(j):
        return lax.rem(me + GROUP - j, GROUP)

    def member(m):
        return (z * GROUP + m, strip)

    place = me * 4 + strip

    def in_plane(d):
        return (z * GROUP + d // 4, lax.rem(d, 4))

    up_id = (layer - GROUP, strip)
    down_id = (layer + GROUP, strip)

    copies = [
        pltpu.make_async_copy(probes, inbuf, in_sem.at[0]),
        pltpu.make_async_copy(slow, slowbuf, in_sem.at[1]),
        pltpu.make_async_copy(absorb, flags, in_sem.at[2]),
        pltpu.make_async_copy(partition.at[pl.ds(16 * z, 16)], points, in_sem.at[3]),
    ]
    for c in copies:
        c.start()

    barrier = pltpu.get_barrier_semaphore()
    for j in range(1, PLANE):
        pl.semaphore_signal(barrier, inc=1, device_id=in_plane(lax.rem(place + j, PLANE)), device_id_type=MESH)

    def meets(other):
        return (z == 3) | (z == 4) | (other == 3) | (other == 4) | (other == z + 1) | (other == z - 1)

    greeted = PLANE - 1
    for dz in range(1, 8):
        other = lax.rem(z + dz, 8)
        greeted = greeted + jnp.where(meets(other), 1, 0)

        @pl.when(meets(other))
        def _():
            pl.semaphore_signal(barrier, inc=1, device_id=(other * GROUP + me, strip), device_id_type=MESH)

    @pl.when(strip == 0)
    def _():
        erecv[0] = jnp.zeros_like(erecv[0])

    @pl.when(strip == 3)
    def _():
        erecv[1] = jnp.zeros_like(erecv[1])

    @pl.when(z == 0)
    def _():
        for p in range(PAIR):
            fbuf[p, 0:HALO] = jnp.zeros((HALO, 2, MAIN, 8, 128), F32)
        sbuf[0:HALO] = jnp.zeros((HALO, 6, 8, 128), F32)

    @pl.when(z == 7)
    def _():
        for p in range(PAIR):
            fbuf[p, HALO + OWN : ROWS] = jnp.zeros((HALO, 2, MAIN, 8, 128), F32)
        sbuf[HALO + OWN : ROWS] = jnp.zeros((HALO, 6, 8, 128), F32)

    for c in copies:
        c.wait()

    for side, chunk in ((0, 0), (1, 31)):
        for r in range(2):
            at = 2 * chunk + r
            for q in range(4):
                esend[side, r, 8 * q : 8 * q + 8, :] = inbuf[pl.ds(512 * q + at, 8, stride=64), :]
            esend[side, r, 32:40, :] = jnp.broadcast_to(slowbuf[at : at + 1, :], (8, 128))

    pl.semaphore_wait(barrier, greeted)

    def edge_copy(side, to):
        return pltpu.make_async_remote_copy(
            src_ref=esend.at[side], dst_ref=erecv.at[1 - side], send_sem=es.at[side], recv_sem=er.at[1 - side],
            device_id=(layer, to), device_id_type=MESH,
        )

    @pl.when(strip > 0)
    def _():
        edge_copy(0, strip - 1).start()

    @pl.when(strip < 3)
    def _():
        edge_copy(1, strip + 1).start()

    def rows_of(m):
        return pl.ds(HALO + 2 * m, 2)

    def f_copy(p, j, dst_member, to):
        return pltpu.make_async_remote_copy(
            src_ref=sendf.at[p, to], dst_ref=fbuf.at[p, rows_of(dst_member)], send_sem=fs.at[p, j], recv_sem=fr.at[p, j],
            device_id=member(to), device_id_type=MESH,
        )

    def s_copy(j, dst_member, to):
        return pltpu.make_async_remote_copy(
            src_ref=ssend.at[to], dst_ref=sbuf.at[rows_of(dst_member)], send_sem=fs.at[2, j], recv_sem=fr.at[2, j],
            device_id=member(to), device_id_type=MESH,
        )

    def own_f(p):
        return pltpu.make_async_copy(sendf.at[p, me], fbuf.at[p, rows_of(me)], own_sem.at[p])

    own_s = pltpu.make_async_copy(ssend.at[me], sbuf.at[rows_of(me)], own_sem.at[2])

    def stage_f(p):
        for m in range(GROUP):
            for r in range(2):
                for c in range(2):
                    for t in range(MAIN):
                        base = ((2 * m + p) * 2 + c) * 64 + 2 * t + r
                        sendf[p, m, r, c, t] = inbuf[pl.ds(base, 8, stride=8), :]

    def stage_s():
        sub = sublanes()
        for r in range(2):
            flag = jnp.full((8, 128), flags[r], jnp.int32).astype(F32)
            tiles = [slowbuf[pl.ds(2 * t + r, 8, stride=8), :] for t in range(MAIN)]
            for m in range(GROUP):
                for t in range(MAIN):
                    ssend[m, r, t] = tiles[t]
                for side in range(2):
                    mine = erecv[side, r, 4 * m : 4 * m + 8, :]
                    there = erecv[side, r, 32:40, :]
                    ssend[m, r, MAIN + side] = jnp.where(sub < 4, mine, jnp.where(sub == 4, there, flag))

    def send_f(p):
        stage_f(p)
        for j in range(1, GROUP):
            f_copy(p, j, me, peer_of(j)).start()
        own_f(p).start()

    send_f(0)

    @pl.when(strip > 0)
    def _():
        edge_copy(0, strip - 1).wait_send()

    @pl.when(strip > 0)
    def _():
        edge_copy(1, strip - 1).wait_recv()

    @pl.when(strip < 3)
    def _():
        edge_copy(1, strip + 1).wait_send()
        edge_copy(0, strip + 1).wait_recv()

    stage_s()
    for j in range(1, GROUP):
        s_copy(j, me, peer_of(j)).start()
    own_s.start()
    send_f(1)

    def forward_ref(k, rows):
        return sbuf.at[rows] if k == 2 else fbuf.at[k, rows]

    def up_copy(k, j, m):
        return pltpu.make_async_remote_copy(
            src_ref=forward_ref(k, rows_of(m)), dst_ref=forward_ref(k, pl.ds(HALO + OWN + 2 * m, 2)),
            send_sem=zs.at[k, j], recv_sem=zr.at[k, j], device_id=up_id, device_id_type=MESH,
        )

    def down_copy(k, j, m):
        return pltpu.make_async_remote_copy(
            src_ref=forward_ref(k, rows_of(m)), dst_ref=forward_ref(k, pl.ds(2 * (m - 4), 2)),
            send_sem=zs.at[k, j], recv_sem=zr.at[k, j], device_id=down_id, device_id_type=MESH,
        )

    def arrive(k, j):
        m = from_of(j)
        if j == 0:
            (own_s if k == 2 else own_f(k)).wait()
        elif k == 2:
            s_copy(j, m, peer_of(j)).wait_recv()
        else:
            f_copy(k, j, m, peer_of(j)).wait_recv()

        @pl.when((m < 4) & (z > 0))
        def _():
            up_copy(k, j, m).start()

        @pl.when((m >= 4) & (z < 7))
        def _():
            down_copy(k, j, m).start()

    def halo_wait(k):
        for j in range(GROUP):
            m = from_of(j)

            @pl.when((m < 4) & (z < 7))
            def _():
                up_copy(k, j, m).wait_recv()

            @pl.when((m >= 4) & (z > 0))
            def _():
                down_copy(k, j, m).wait_recv()

    for j in range(GROUP):
        arrive(0, j)
    for j in range(GROUP):
        arrive(2, j)
    halo_wait(2)

    def coef_row(r, carry):
        tiles = [sbuf[r, t] for t in range(MAIN)]
        left, right = sbuf[r, MAIN], sbuf[r, MAIN + 1]
        flag = jnp.broadcast_to(left[5:6, :], (8, 128))
        wide = widen(tiles, jnp.broadcast_to(left[4:5, :], (8, 128)), jnp.broadcast_to(right[4:5, :], (8, 128)))
        lane, sub = lanes(), sublanes()
        inside = ((r >= HALO) | (z > 0)) & ((r < HALO + OWN) | (z < 7))
        for t in range(WIDE):
            dre = 4.0 - wide[t]
            dim = BETA * wide[t] + SIGMA * flag
            scale = OMEGA / (dre * dre + dim * dim)
            keep = jnp.full((8, 128), inside)
            if t == 0:
                keep = keep & ((lane >= 64) | (sub > 0) | jnp.full((8, 128), strip > 0))
            if t == WIDE - 1:
                keep = keep & ((lane < 64) | (sub < 7) | jnp.full((8, 128), strip < 3))
            coef[r, 0, t] = jnp.where(keep, dre * scale, 0.0)
            coef[r, 1, t] = jnp.where(keep, -dim * scale, 0.0)
        return carry

    lax.fori_loop(0, ROWS, coef_row, 0)
    halo_wait(0)

    def source_row(p):
        def body(r, carry):
            left, right = sbuf[r, MAIN], sbuf[r, MAIN + 1]
            wide = []
            for c in range(2):
                at = 2 * p + c
                wide.append(
                    widen(
                        [fbuf[p, r, c, t] for t in range(MAIN)],
                        jnp.broadcast_to(left[at : at + 1, :], (8, 128)),
                        jnp.broadcast_to(right[at : at + 1, :], (8, 128)),
                    )
                )
            for t in range(WIDE):
                er_, ei_ = coef[r, 0, t], coef[r, 1, t]
                fr_, fi_ = wide[0][t], wide[1][t]
                gbuf[p, r, 0, t] = er_ * fr_ - ei_ * fi_
                gbuf[p, r, 1, t] = er_ * fi_ + ei_ * fr_
            return carry

        lax.fori_loop(0, ROWS, body, 0)

    def relaxed(p, r, above, here, below):
        near = beside(here[:WIDE]) + beside(here[WIDE:])
        re, im = [], []
        for t in range(WIDE):
            er_, ei_ = coef[r, 0, t], coef[r, 1, t]
            nr = above[t] + below[t] + near[t]
            ni = above[WIDE + t] + below[WIDE + t] + near[WIDE + t]
            re.append((1.0 - OMEGA) * here[t] + gbuf[p, r, 0, t] + (er_ * nr - ei_ * ni))
            im.append((1.0 - OMEGA) * here[WIDE + t] + gbuf[p, r, 1, t] + (er_ * ni + ei_ * nr))
        return re + im

    def load(ref, p, r):
        return [ref[p, r, c, t] for c in range(2) for t in range(WIDE)]

    def store(p, r, row):
        for c in range(2):
            for t in range(WIDE):
                ubuf[p, r, c, t] = row[c * WIDE + t]

    def sweep(p, step):
        src = gbuf if step == 2 else ubuf
        low, high = step - 1, ROWS + 1 - step

        def body(i, carry):
            r = low + 2 * i
            above, here = carry[: 2 * WIDE], carry[2 * WIDE :]
            below = load(src, p, r + 1)
            new = relaxed(p, r, above, here, below)
            after = load(src, p, r + 2)
            if step < ITERS:
                store(p, r, new)
            new2 = relaxed(p, r + 1, here, below, after)
            if step < ITERS:
                store(p, r + 1, new2)
            else:
                for rr_, row in ((r, new), (r + 1, new2)):
                    for c in range(2):
                        tiles = narrow(row[c * WIDE : (c + 1) * WIDE])
                        for t in range(MAIN):
                            obuf[p, rr_ - HALO, c, t] = tiles[t]
            return tuple(below) + tuple(after)

        lax.fori_loop(0, (high - low) // 2, body, tuple(load(src, p, low - 1)) + tuple(load(src, p, low)))

    def back_copy(p, j, of_member, to):
        return pltpu.make_async_remote_copy(
            src_ref=obuf.at[p, pl.ds(2 * to, 2)], dst_ref=rbuf.at[2 * of_member + p], send_sem=rs.at[p, j], recv_sem=rr.at[p, j],
            device_id=member(to), device_id_type=MESH,
        )

    def own_back(p):
        return pltpu.make_async_copy(obuf.at[p, pl.ds(2 * me, 2)], rbuf.at[2 * me + p], own_sem.at[3 + p])

    def send_back(p):
        for j in range(1, GROUP):
            back_copy(p, j, me, peer_of(j)).start()
        own_back(p).start()

    def out_copy(p, j):
        at = pl.ds((2 * from_of(j) + p) * 128, 128)
        return pltpu.make_async_copy(outbuf.at[at], field.at[at], out_sem.at[p, j])

    def receive_back(p):
        for j in range(GROUP):
            m = from_of(j)
            if j == 0:
                own_back(p).wait()
            else:
                back_copy(p, j, m, peer_of(j)).wait_recv()
            q = 2 * m + p
            for r in range(2):
                for c in range(2):
                    for t in range(MAIN):
                        outbuf[pl.ds((q * 2 + c) * 64 + 2 * t + r, 8, stride=8), :] = rbuf[q, r, c, t]
            out_copy(p, j).start()

    def trace_copy(side, p, other):
        return pltpu.make_async_remote_copy(
            src_ref=obuf.at[p, OWN - 1 if side == 0 else 0], dst_ref=tbuf.at[side, p],
            send_sem=ts.at[p, other], recv_sem=tr.at[side, p],
            device_id=(other * GROUP + me, strip), device_id_type=MESH,
        )

    def trace_own(side, p):
        return pltpu.make_async_copy(obuf.at[p, OWN - 1 if side == 0 else 0], tbuf.at[side, p], town.at[p])

    def trace_send(p):
        for side in range(2):
            owner = 3 + side

            @pl.when(z == owner)
            def _():
                for other in range(8):
                    if other == owner:
                        trace_own(side, p).start()
                    else:
                        trace_copy(side, p, other).start()

    def trace_wait(p):
        for side in range(2):
            owner = 3 + side

            @pl.when(z == owner)
            def _():
                trace_own(side, p).wait()

            @pl.when(z != owner)
            def _():
                trace_copy(side, p, 0).wait_recv()

    def pick(g, carry):
        sub = sublanes()
        at = jnp.broadcast_to(points[pl.ds(g, 1), :], (8, 128)) - strip * 4096
        tile, lane = (at >> 7) & 3, at & 127
        hit = (at >> 9) == sub
        rows = jnp.zeros((8, 128), F32)
        for side in range(2):
            for p in range(PAIR):
                for c in range(2):
                    got = [jnp.take_along_axis(tbuf[side, p, c, t], lane, axis=1) for t in range(MAIN)]
                    best = got[0]
                    for t in range(1, MAIN):
                        best = jnp.where(tile == t, got[t], best)
                    one = jnp.sum(jnp.where(hit, best, 0.0), axis=0, keepdims=True)
                    rows = jnp.where(sub == side * 4 + p * 2 + c, jnp.broadcast_to(one, (8, 128)), rows)
        picked[g] = rows
        return carry

    def picked_copy(j, source, to):
        return pltpu.make_async_remote_copy(
            src_ref=picked.at[to // 2], dst_ref=gat.at[source], send_sem=gs.at[j], recv_sem=gr.at[j],
            device_id=in_plane(to), device_id_type=MESH,
        )

    picked_own = pltpu.make_async_copy(picked.at[place // 2], gat.at[place], gown)

    def pick_send():
        lax.fori_loop(0, 16, pick, 0)
        for j in range(1, PLANE):
            picked_copy(j, place, lax.rem(place + j, PLANE)).start()
        picked_own.start()

    def compress():
        for j in range(1, PLANE):
            picked_copy(j, lax.rem(place + PLANE - j, PLANE), lax.rem(place + j, PLANE)).wait_recv()
        picked_own.wait()
        lane32 = lax.broadcasted_iota(jnp.int32, (32, 128), 1)
        row32 = lax.broadcasted_iota(jnp.int32, (32, 128), 0)
        odd = jnp.full((8, 128), lax.rem(strip, 2) == 1)
        for m in range(GROUP):
            tile = (gat[4 * m] + gat[4 * m + 1]) + (gat[4 * m + 2] + gat[4 * m + 3])
            tile = jnp.where(odd, pltpu.roll(tile, 64, 1), tile)
            tile = jnp.where(lanes() < 64, tile, 0.0)
            for side in range(2):
                mats[side, 4 * m : 4 * m + 4, :] = tile[4 * side : 4 * side + 4, :]
        augmented = []
        for side in range(2):
            mat = mats[side]
            zero = jnp.zeros((32, 128), F32)
            spread = jnp.concatenate([zero, zero, mat, zero], axis=0)
            gram = lax.dot_general(
                mat, spread, (((1,), (1,)), ((), ())), precision=lax.Precision.HIGHEST, preferred_element_type=F32
            )
            augmented.append(jnp.where(lane32 < 64, mat, gram))
        for k in range(32):
            for side in range(2):
                a = augmented[side]
                inverse = lax.rsqrt(a[k : k + 1, 64 + k : 65 + k])
                row = a[k : k + 1, :] * inverse
                column = a[:, 64 + k : 65 + k] * inverse
                less = a - column * row
                augmented[side] = jnp.where(row32 > k, less, jnp.where(row32 == k, jnp.broadcast_to(row, (32, 128)), a))
        for side in range(2):
            based[side] = augmented[side][:, :BS]
        pltpu.make_async_copy(based, bases, base_sem).start()

    source_row(0)
    for step in range(2, ITERS + 1):
        sweep(0, step)
        arrive(1, step - 2)
    trace_send(0)
    send_back(0)
    halo_wait(1)
    source_row(1)
    for step in range(2, ITERS + 1):
        sweep(1, step)
    trace_send(1)
    send_back(1)
    trace_wait(0)
    receive_back(0)
    trace_wait(1)
    pick_send()
    compress()
    receive_back(1)

    for j in range(1, GROUP):
        for p in range(PAIR):
            f_copy(p, j, me, peer_of(j)).wait_send()
            back_copy(p, j, me, peer_of(j)).wait_send()
        s_copy(j, me, peer_of(j)).wait_send()
    for k in range(3):
        for j in range(GROUP):
            m = from_of(j)

            @pl.when((m < 4) & (z > 0))
            def _():
                up_copy(k, j, m).wait_send()

            @pl.when((m >= 4) & (z < 7))
            def _():
                down_copy(k, j, m).wait_send()

    for p in range(PAIR):
        for side in range(2):

            @pl.when(z == 3 + side)
            def _():
                for other in range(8):
                    if other != 3 + side:
                        trace_copy(side, p, other).wait_send()

    for j in range(1, PLANE):
        picked_copy(j, place, lax.rem(place + j, PLANE)).wait_send()
    for p in range(PAIR):
        for j in range(GROUP):
            out_copy(p, j).wait()
    pltpu.make_async_copy(based, bases, base_sem).wait()


def swept(probes, slow, absorb, partition):
    any_space = pl.BlockSpec(memory_space=pl.ANY)
    dma = pltpu.SemaphoreType.DMA
    return pl.pallas_call(
        kernel,
        out_shape=(
            jax.ShapeDtypeStruct((2 * PROBES * 64, 128), F32),
            jax.ShapeDtypeStruct((2, 2 * PROBES, BS), F32),
        ),
        in_specs=[any_space] * 4,
        out_specs=(any_space, any_space),
        scratch_shapes=[
            pltpu.VMEM((2 * PROBES * 64, 128), F32),
            pltpu.VMEM((64, 128), F32),
            pltpu.SMEM((2,), jnp.int32),
            pltpu.VMEM((2, 2, 40, 128), F32),
            pltpu.VMEM((2, 2, 40, 128), F32),
            pltpu.VMEM((PAIR, GROUP, 2, 2, MAIN, 8, 128), F32),
            pltpu.VMEM((GROUP, 2, 6, 8, 128), F32),
            pltpu.VMEM((PAIR, ROWS, 2, MAIN, 8, 128), F32),
            pltpu.VMEM((ROWS, 6, 8, 128), F32),
            pltpu.VMEM((ROWS, 2, WIDE, 8, 128), F32),
            pltpu.VMEM((PAIR, ROWS, 2, WIDE, 8, 128), F32),
            pltpu.VMEM((PAIR, ROWS, 2, WIDE, 8, 128), F32),
            pltpu.VMEM((PAIR, OWN, 2, MAIN, 8, 128), F32),
            pltpu.VMEM((PROBES, 2, 2, MAIN, 8, 128), F32),
            pltpu.VMEM((2 * PROBES * 64, 128), F32),
            pltpu.VMEM((16, 128), jnp.int32),
            pltpu.VMEM((2, PAIR, 2, MAIN, 8, 128), F32),
            pltpu.VMEM((16, 8, 128), F32),
            pltpu.VMEM((PLANE, 8, 128), F32),
            pltpu.VMEM((2, 32, 128), F32),
            pltpu.VMEM((2, 32, BS), F32),
            dma((4,)),
            dma((2,)),
            dma((2,)),
            dma((5,)),
            dma((3, GROUP)),
            dma((3, GROUP)),
            dma((3, GROUP)),
            dma((3, GROUP)),
            dma((PAIR, GROUP)),
            dma((PAIR, GROUP)),
            dma((PAIR, GROUP)),
            dma((PAIR, 8)),
            dma((2, PAIR)),
            dma((PAIR,)),
            dma((PLANE,)),
            dma((PLANE,)),
            dma(()),
            dma(()),
        ],
        compiler_params=pltpu.CompilerParams(
            collective_id=1, has_side_effects=True, vmem_limit_bytes=48 * 1024 * 1024
        ),
        name="sweeps",
    )(probes, slow, absorb, partition)


def per_device(probes, slowness, absorbing, partition):
    flat = probes.reshape(PROBES, 2, 2, 32, 128).transpose(0, 1, 3, 2, 4).reshape(2 * PROBES * 64, 128)
    slow = slowness.reshape(2, 32, 128).transpose(1, 0, 2).reshape(64, 128)
    out, bases = swept(flat, slow, absorbing, partition.reshape(128, 128))
    field = out.reshape(PROBES, 2, 32, 2, 128).transpose(0, 1, 3, 2, 4).reshape(PROBES, 2, 2, 4096)
    return field, bases[None]


def solution(mesh):
    return jax.shard_map(
        per_device,
        mesh=mesh,
        in_specs=(P(None, None, "layer", "strip"), P("layer", "strip"), P("layer"), P()),
        out_specs=(P(None, None, "layer", "strip"), P(("layer", "strip"), None, None, None)),
        check_vma=False,
    )
```

time: 1030 us -> 91.1 us (0.09)
  the two profiles are of different devices: /device:TPU:16 before, /device:TPU:1 now
where the time goes in v1:
time: 91.1 us; the launch traced here: 90.9 us
  Pallas kernels  85.2 us (94%)
  local copies, waits for them, and re-layouts  5.06 us (6%)
    pallas_call x1, Pallas kernels, swept(): pl.pallas_call(kernel, out_shape=(jax.ShapeDtypeStruct((2 * PROBES * 64,...  85.2 us
    unnamed x10, local copies, waits for them, and re-layouts  5.06 us

profile of v1, /device:TPU:1, one launch (start us, length us, event | category | flops | bytes accessed | tf_op | source)
XLA Modules:
  0.0 90.9 jit_solution(17199138313148895638)
XLA Ops:
  0.6 0.0 copy-start.3
  0.6 0.6 copy-done.3
  1.3 0.0 copy-start
  1.3 1.2 %copy-done = f32[16,2,2,4096]{3,2,1,0:T(2,128)S(1)} copy-done((f32[16,2,2,4096]{3,2,1,0:T(2,128)S(1)}, f32[16,2,2,4096]{3,2,1,0:T(2,128)}, u32[]{:S(2)}) %copy-start) | copy-done | bytes 1048600
  2.5 0.0 copy-start.1
  2.5 0.8 copy-done.1
  3.4 0.0 copy-start.2
  3.4 0.8 copy-done.2
  4.1 85.2 %sweeps.1 = (f32[2048,128]{1,0:T(8,128)S(1)}, f32[2,32,64]{2,1,0:T(8,128)S(1)}) custom-call(f32[2048,128]{1,0:T(8,128)S(1)} %bitcast.17, f32[64,128]{1,0:T(8,128)S(1)} %bitcast.20, s32[2]{0:T(128)S(1)} %copy-done.3, s32[128,128]{1,0:T(8,128)S(1)} %bitcast.19), custom_call_target="tpu_custom_call" | custom-call | tf_op jit(solution)/shard_map/sweeps/pallas_call | solution.py:562
  89.3 1.0 %copy.11 = f32[16,2,2,4096]{3,2,1,0:T(2,128)} copy(f32[16,2,2,4096]{3,2,1,0:T(2,128)S(1)} %bitcast.18) | data formatting | bytes 2097152
  90.3 0.6 copy.12
Async XLA Ops:
  0.6 0.7 copy-start.3
  1.3 1.2 %copy-start = (f32[16,2,2,4096]{3,2,1,0:T(2,128)S(1)}, f32[16,2,2,4096]{3,2,1,0:T(2,128)}, u32[]{:S(2)}) copy-start(f32[16,2,2,4096]{3,2,1,0:T(2,128)} %param.4) | copy-start | bytes 3145732
  2.5 0.8 copy-start.1
  3.4 0.8 copy-start.2

commit v2 on v1

--- a/solution.py
+++ b/solution.py
@@ -9,6 +9,7 @@
 
 ITERS = 9
 BS = 64
+BLOCK = 8
 OMEGA = 0.8
 BETA = 0.5
 SIGMA = 1.5
@@ -24,6 +25,7 @@
 MAIN = 4
 WIDE = 5
 F32 = jnp.float32
+VMEM_LIMIT = 62 * 1024 * 1024
 
 
 def lanes():
@@ -66,10 +68,10 @@
 def kernel(
     probes, slow, absorb, partition,
     field, bases,
-    inbuf, slowbuf, flags, esend, erecv, sendf, ssend, fbuf, sbuf, coef, gbuf, ubuf, obuf, rbuf, outbuf,
-    points, tbuf, picked, gat, mats, based,
-    in_sem, es, er, own_sem, fs, fr, zs, zr, rs, rr, out_sem,
-    ts, tr, town, gs, gr, gown, base_sem,
+    inbuf, slowbuf, flags, esend, erecv, sendf, ssend, epack, fbuf, sbuf, ebuf, coef, gbuf, ubuf, vbuf, obuf, rbuf,
+    points, tbuf, picked, gat, mats,
+    in_sem, es, er, own_sem, fs, fr, zs, zr, rs, rr,
+    ts, tr, town, gs, gr, gown,
 ):
     layer = lax.axis_index("layer")
     strip = lax.axis_index("strip")
@@ -130,13 +132,15 @@
     def _():
         for p in range(PAIR):
             fbuf[p, 0:HALO] = jnp.zeros((HALO, 2, MAIN, 8, 128), F32)
-        sbuf[0:HALO] = jnp.zeros((HALO, 6, 8, 128), F32)
+        sbuf[0:HALO] = jnp.zeros((HALO, MAIN, 8, 128), F32)
+        ebuf[0:HALO] = jnp.zeros((HALO, 2, 8, 128), F32)
 
     @pl.when(z == 7)
     def _():
         for p in range(PAIR):
             fbuf[p, HALO + OWN : ROWS] = jnp.zeros((HALO, 2, MAIN, 8, 128), F32)
-        sbuf[HALO + OWN : ROWS] = jnp.zeros((HALO, 6, 8, 128), F32)
+        sbuf[HALO + OWN : ROWS] = jnp.zeros((HALO, MAIN, 8, 128), F32)
+        ebuf[HALO + OWN : ROWS] = jnp.zeros((HALO, 2, 8, 128), F32)
 
     for c in copies:
         c.wait()
@@ -175,14 +179,21 @@
 
     def s_copy(j, dst_member, to):
         return pltpu.make_async_remote_copy(
-            src_ref=ssend.at[to], dst_ref=sbuf.at[rows_of(dst_member)], send_sem=fs.at[2, j], recv_sem=fr.at[2, j],
+            src_ref=ssend, dst_ref=sbuf.at[rows_of(dst_member)], send_sem=fs.at[2, j], recv_sem=fr.at[2, j],
+            device_id=member(to), device_id_type=MESH,
+        )
+
+    def e_copy(j, dst_member, to):
+        return pltpu.make_async_remote_copy(
+            src_ref=epack.at[to], dst_ref=ebuf.at[rows_of(dst_member)], send_sem=fs.at[3, j], recv_sem=fr.at[3, j],
             device_id=member(to), device_id_type=MESH,
         )
 
     def own_f(p):
         return pltpu.make_async_copy(sendf.at[p, me], fbuf.at[p, rows_of(me)], own_sem.at[p])
 
-    own_s = pltpu.make_async_copy(ssend.at[me], sbuf.at[rows_of(me)], own_sem.at[2])
+    own_s = pltpu.make_async_copy(ssend, sbuf.at[rows_of(me)], own_sem.at[2])
+    own_e = pltpu.make_async_copy(epack.at[me], ebuf.at[rows_of(me)], own_sem.at[5])
 
     def stage_f(p):
         for m in range(GROUP):
@@ -193,17 +204,19 @@
                         sendf[p, m, r, c, t] = inbuf[pl.ds(base, 8, stride=8), :]
 
     def stage_s():
+        for r in range(2):
+            for t in range(MAIN):
+                ssend[r, t] = slowbuf[pl.ds(2 * t + r, 8, stride=8), :]
+
+    def stage_e():
         sub = sublanes()
         for r in range(2):
             flag = jnp.full((8, 128), flags[r], jnp.int32).astype(F32)
-            tiles = [slowbuf[pl.ds(2 * t + r, 8, stride=8), :] for t in range(MAIN)]
             for m in range(GROUP):
-                for t in range(MAIN):
-                    ssend[m, r, t] = tiles[t]
                 for side in range(2):
                     mine = erecv[side, r, 4 * m : 4 * m + 8, :]
                     there = erecv[side, r, 32:40, :]
-                    ssend[m, r, MAIN + side] = jnp.where(sub < 4, mine, jnp.where(sub == 4, there, flag))
+                    epack[m, r, side] = jnp.where(sub < 4, mine, jnp.where(sub == 4, there, flag))
 
     def send_f(p):
         stage_f(p)
@@ -212,28 +225,28 @@
         own_f(p).start()
 
     send_f(0)
-
-    @pl.when(strip > 0)
-    def _():
-        edge_copy(0, strip - 1).wait_send()
-
-    @pl.when(strip > 0)
-    def _():
-        edge_copy(1, strip - 1).wait_recv()
-
-    @pl.when(strip < 3)
-    def _():
-        edge_copy(1, strip + 1).wait_send()
-        edge_copy(0, strip + 1).wait_recv()
-
     stage_s()
     for j in range(1, GROUP):
         s_copy(j, me, peer_of(j)).start()
     own_s.start()
-    send_f(1)
+
+    @pl.when(strip > 0)
+    def _():
+        edge_copy(0, strip - 1).wait_send()
+        edge_copy(1, strip - 1).wait_recv()
+
+    @pl.when(strip < 3)
+    def _():
+        edge_copy(1, strip + 1).wait_send()
+        edge_copy(0, strip + 1).wait_recv()
+
+    stage_e()
+    for j in range(1, GROUP):
+        e_copy(j, me, peer_of(j)).start()
+    own_e.start()
 
     def forward_ref(k, rows):
-        return sbuf.at[rows] if k == 2 else fbuf.at[k, rows]
+        return (ebuf if k == 3 else sbuf).at[rows] if k >= 2 else fbuf.at[k, rows]
 
     def up_copy(k, j, m):
         return pltpu.make_async_remote_copy(
@@ -250,9 +263,11 @@
     def arrive(k, j):
         m = from_of(j)
         if j == 0:
-            (own_s if k == 2 else own_f(k)).wait()
+            (own_e if k == 3 else own_s if k == 2 else own_f(k)).wait()
         elif k == 2:
             s_copy(j, m, peer_of(j)).wait_recv()
+        elif k == 3:
+            e_copy(j, m, peer_of(j)).wait_recv()
         else:
             f_copy(k, j, m, peer_of(j)).wait_recv()
 
@@ -280,11 +295,23 @@
         arrive(0, j)
     for j in range(GROUP):
         arrive(2, j)
+    send_f(1)
+    for j in range(GROUP):
+        arrive(3, j)
     halo_wait(2)
-
-    def coef_row(r, carry):
+    halo_wait(3)
+
+    def by_rows(work):
+        def four(i, carry):
+            for n in range(4):
+                work(4 * i + n)
+            return carry
+
+        lax.fori_loop(0, ROWS // 4, four, 0)
+
+    def coef_row(r):
         tiles = [sbuf[r, t] for t in range(MAIN)]
-        left, right = sbuf[r, MAIN], sbuf[r, MAIN + 1]
+        left, right = ebuf[r, 0], ebuf[r, 1]
         flag = jnp.broadcast_to(left[5:6, :], (8, 128))
         wide = widen(tiles, jnp.broadcast_to(left[4:5, :], (8, 128)), jnp.broadcast_to(right[4:5, :], (8, 128)))
         lane, sub = lanes(), sublanes()
@@ -300,14 +327,13 @@
                 keep = keep & ((lane < 64) | (sub < 7) | jnp.full((8, 128), strip < 3))
             coef[r, 0, t] = jnp.where(keep, dre * scale, 0.0)
             coef[r, 1, t] = jnp.where(keep, -dim * scale, 0.0)
-        return carry
-
-    lax.fori_loop(0, ROWS, coef_row, 0)
+
+    by_rows(coef_row)
     halo_wait(0)
 
     def source_row(p):
-        def body(r, carry):
-            left, right = sbuf[r, MAIN], sbuf[r, MAIN + 1]
+        def body(r):
+            left, right = ebuf[r, 0], ebuf[r, 1]
             wide = []
             for c in range(2):
                 at = 2 * p + c
@@ -323,9 +349,8 @@
                 fr_, fi_ = wide[0][t], wide[1][t]
                 gbuf[p, r, 0, t] = er_ * fr_ - ei_ * fi_
                 gbuf[p, r, 1, t] = er_ * fi_ + ei_ * fr_
-            return carry
-
-        lax.fori_loop(0, ROWS, body, 0)
+
+        by_rows(body)
 
     def relaxed(p, r, above, here, below):
         near = beside(here[:WIDE]) + beside(here[WIDE:])
@@ -341,35 +366,31 @@
     def load(ref, p, r):
         return [ref[p, r, c, t] for c in range(2) for t in range(WIDE)]
 
-    def store(p, r, row):
-        for c in range(2):
-            for t in range(WIDE):
-                ubuf[p, r, c, t] = row[c * WIDE + t]
-
     def sweep(p, step):
-        src = gbuf if step == 2 else ubuf
-        low, high = step - 1, ROWS + 1 - step
+        src = gbuf if step == 2 else (ubuf if step % 2 else vbuf)
+        dst = vbuf if step % 2 else ubuf
+        low, count = step - 1, ROWS + 2 - 2 * step
+        block = {30: 10, 28: 7, 26: 13, 24: 8, 22: 11, 20: 10, 18: 9, 16: 8}[count]
 
         def body(i, carry):
-            r = low + 2 * i
-            above, here = carry[: 2 * WIDE], carry[2 * WIDE :]
-            below = load(src, p, r + 1)
-            new = relaxed(p, r, above, here, below)
-            after = load(src, p, r + 2)
-            if step < ITERS:
-                store(p, r, new)
-            new2 = relaxed(p, r + 1, here, below, after)
-            if step < ITERS:
-                store(p, r + 1, new2)
-            else:
-                for rr_, row in ((r, new), (r + 1, new2)):
+            above, here = list(carry[: 2 * WIDE]), list(carry[2 * WIDE :])
+            for n in range(block):
+                r = low + block * i + n
+                below = load(src, p, r + 1)
+                new = relaxed(p, r, above, here, below)
+                if step < ITERS:
                     for c in range(2):
-                        tiles = narrow(row[c * WIDE : (c + 1) * WIDE])
+                        for t in range(WIDE):
+                            dst[p, r, c, t] = new[c * WIDE + t]
+                else:
+                    for c in range(2):
+                        tiles = narrow(new[c * WIDE : (c + 1) * WIDE])
                         for t in range(MAIN):
-                            obuf[p, rr_ - HALO, c, t] = tiles[t]
-            return tuple(below) + tuple(after)
-
-        lax.fori_loop(0, (high - low) // 2, body, tuple(load(src, p, low - 1)) + tuple(load(src, p, low)))
+                            obuf[p, r - HALO, c, t] = tiles[t]
+                above, here = here, below
+            return tuple(above) + tuple(here)
+
+        lax.fori_loop(0, count // block, body, tuple(load(src, p, low - 1)) + tuple(load(src, p, low)))
 
     def back_copy(p, j, of_member, to):
         return pltpu.make_async_remote_copy(
@@ -384,10 +405,6 @@
         for j in range(1, GROUP):
             back_copy(p, j, me, peer_of(j)).start()
         own_back(p).start()
-
-    def out_copy(p, j):
-        at = pl.ds((2 * from_of(j) + p) * 128, 128)
-        return pltpu.make_async_copy(outbuf.at[at], field.at[at], out_sem.at[p, j])
 
     def receive_back(p):
         for j in range(GROUP):
@@ -400,8 +417,7 @@
             for r in range(2):
                 for c in range(2):
                     for t in range(MAIN):
-                        outbuf[pl.ds((q * 2 + c) * 64 + 2 * t + r, 8, stride=8), :] = rbuf[q, r, c, t]
-            out_copy(p, j).start()
+                        field[pl.ds((q * 2 + c) * 64 + 2 * t + r, 8, stride=8), :] = rbuf[q, r, c, t]
 
     def trace_copy(side, p, other):
         return pltpu.make_async_remote_copy(
@@ -437,23 +453,29 @@
             def _():
                 trace_copy(side, p, 0).wait_recv()
 
-    def pick(g, carry):
+    def pick(p, g):
         sub = sublanes()
         at = jnp.broadcast_to(points[pl.ds(g, 1), :], (8, 128)) - strip * 4096
         tile, lane = (at >> 7) & 3, at & 127
         hit = (at >> 9) == sub
-        rows = jnp.zeros((8, 128), F32)
+        rows = jnp.zeros((8, 128), F32) if p == 0 else picked[g]
         for side in range(2):
-            for p in range(PAIR):
-                for c in range(2):
-                    got = [jnp.take_along_axis(tbuf[side, p, c, t], lane, axis=1) for t in range(MAIN)]
-                    best = got[0]
-                    for t in range(1, MAIN):
-                        best = jnp.where(tile == t, got[t], best)
-                    one = jnp.sum(jnp.where(hit, best, 0.0), axis=0, keepdims=True)
-                    rows = jnp.where(sub == side * 4 + p * 2 + c, jnp.broadcast_to(one, (8, 128)), rows)
+            for c in range(2):
+                got = [jnp.take_along_axis(tbuf[side, p, c, t], lane, axis=1) for t in range(MAIN)]
+                best = got[0]
+                for t in range(1, MAIN):
+                    best = jnp.where(tile == t, got[t], best)
+                one = jnp.sum(jnp.where(hit, best, 0.0), axis=0, keepdims=True)
+                rows = jnp.where(sub == side * 4 + p * 2 + c, jnp.broadcast_to(one, (8, 128)), rows)
         picked[g] = rows
-        return carry
+
+    def pick_all(p):
+        def four(i, carry):
+            for n in range(4):
+                pick(p, 4 * i + n)
+            return carry
+
+        lax.fori_loop(0, 4, four, 0)
 
     def picked_copy(j, source, to):
         return pltpu.make_async_remote_copy(
@@ -464,7 +486,7 @@
     picked_own = pltpu.make_async_copy(picked.at[place // 2], gat.at[place], gown)
 
     def pick_send():
-        lax.fori_loop(0, 16, pick, 0)
+        pick_all(1)
         for j in range(1, PLANE):
             picked_copy(j, place, lax.rem(place + j, PLANE)).start()
         picked_own.start()
@@ -491,22 +513,30 @@
                 mat, spread, (((1,), (1,)), ((), ())), precision=lax.Precision.HIGHEST, preferred_element_type=F32
             )
             augmented.append(jnp.where(lane32 < 64, mat, gram))
-        for k in range(32):
-            for side in range(2):
-                a = augmented[side]
-                inverse = lax.rsqrt(a[k : k + 1, 64 + k : 65 + k])
-                row = a[k : k + 1, :] * inverse
-                column = a[:, 64 + k : 65 + k] * inverse
-                less = a - column * row
-                augmented[side] = jnp.where(row32 > k, less, jnp.where(row32 == k, jnp.broadcast_to(row, (32, 128)), a))
+        for first in range(0, 32, BLOCK):
+            spread = [
+                [jnp.broadcast_to(a[:, 64 + k : 65 + k], (32, 128)) for k in range(first, first + BLOCK)] for a in augmented
+            ]
+            for j in range(BLOCK):
+                k = first + j
+                for side in range(2):
+                    a, columns = augmented[side], spread[side]
+                    inverse = lax.rsqrt(jnp.broadcast_to(columns[j][k : k + 1, :], (32, 128)))
+                    row = jnp.broadcast_to(a[k : k + 1, :], (32, 128)) * inverse
+                    column = columns[j] * inverse
+                    augmented[side] = jnp.where(row32 > k, a - column * row, jnp.where(row32 == k, row, a))
+                    for i in range(j + 1, BLOCK):
+                        across = jnp.broadcast_to(columns[i][k : k + 1, :], (32, 128)) * inverse
+                        columns[i] = columns[i] - column * across
         for side in range(2):
-            based[side] = augmented[side][:, :BS]
-        pltpu.make_async_copy(based, bases, base_sem).start()
+            bases[side] = augmented[side][:, :BS]
 
     source_row(0)
     for step in range(2, ITERS + 1):
         sweep(0, step)
-        arrive(1, step - 2)
+        if step in (2, 3):
+            for j in range(4):
+                arrive(1, 4 * (step - 2) + j)
     trace_send(0)
     send_back(0)
     halo_wait(1)
@@ -516,6 +546,7 @@
     trace_send(1)
     send_back(1)
     trace_wait(0)
+    pick_all(0)
     receive_back(0)
     trace_wait(1)
     pick_send()
@@ -527,7 +558,8 @@
             f_copy(p, j, me, peer_of(j)).wait_send()
             back_copy(p, j, me, peer_of(j)).wait_send()
         s_copy(j, me, peer_of(j)).wait_send()
-    for k in range(3):
+        e_copy(j, me, peer_of(j)).wait_send()
+    for k in range(4):
         for j in range(GROUP):
             m = from_of(j)
 
@@ -550,14 +582,11 @@
 
     for j in range(1, PLANE):
         picked_copy(j, place, lax.rem(place + j, PLANE)).wait_send()
-    for p in range(PAIR):
-        for j in range(GROUP):
-            out_copy(p, j).wait()
-    pltpu.make_async_copy(based, bases, base_sem).wait()
 
 
 def swept(probes, slow, absorb, partition):
-    any_space = pl.BlockSpec(memory_space=pl.ANY)
+    far = pl.BlockSpec(memory_space=pltpu.HBM)
+    near = pl.BlockSpec(memory_space=pltpu.VMEM)
     dma = pltpu.SemaphoreType.DMA
     return pl.pallas_call(
         kernel,
@@ -565,8 +594,8 @@
             jax.ShapeDtypeStruct((2 * PROBES * 64, 128), F32),
             jax.ShapeDtypeStruct((2, 2 * PROBES, BS), F32),
         ),
-        in_specs=[any_space] * 4,
-        out_specs=(any_space, any_space),
+        in_specs=[far] * 4,
+        out_specs=(near, near),
         scratch_shapes=[
             pltpu.VMEM((2 * PROBES * 64, 128), F32),
             pltpu.VMEM((64, 128), F32),
@@ -574,30 +603,30 @@
             pltpu.VMEM((2, 2, 40, 128), F32),
             pltpu.VMEM((2, 2, 40, 128), F32),
             pltpu.VMEM((PAIR, GROUP, 2, 2, MAIN, 8, 128), F32),
-            pltpu.VMEM((GROUP, 2, 6, 8, 128), F32),
+            pltpu.VMEM((2, MAIN, 8, 128), F32),
+            pltpu.VMEM((GROUP, 2, 2, 8, 128), F32),
             pltpu.VMEM((PAIR, ROWS, 2, MAIN, 8, 128), F32),
-            pltpu.VMEM((ROWS, 6, 8, 128), F32),
+            pltpu.VMEM((ROWS, MAIN, 8, 128), F32),
+            pltpu.VMEM((ROWS, 2, 8, 128), F32),
             pltpu.VMEM((ROWS, 2, WIDE, 8, 128), F32),
+            pltpu.VMEM((PAIR, ROWS, 2, WIDE, 8, 128), F32),
             pltpu.VMEM((PAIR, ROWS, 2, WIDE, 8, 128), F32),
             pltpu.VMEM((PAIR, ROWS, 2, WIDE, 8, 128), F32),
             pltpu.VMEM((PAIR, OWN, 2, MAIN, 8, 128), F32),
             pltpu.VMEM((PROBES, 2, 2, MAIN, 8, 128), F32),
-            pltpu.VMEM((2 * PROBES * 64, 128), F32),
             pltpu.VMEM((16, 128), jnp.int32),
             pltpu.VMEM((2, PAIR, 2, MAIN, 8, 128), F32),
             pltpu.VMEM((16, 8, 128), F32),
             pltpu.VMEM((PLANE, 8, 128), F32),
             pltpu.VMEM((2, 32, 128), F32),
-            pltpu.VMEM((2, 32, BS), F32),
             dma((4,)),
             dma((2,)),
             dma((2,)),
-            dma((5,)),
-            dma((3, GROUP)),
-            dma((3, GROUP)),
-            dma((3, GROUP)),
-            dma((3, GROUP)),
-            dma((PAIR, GROUP)),
+            dma((6,)),
+            dma((4, GROUP)),
+            dma((4, GROUP)),
+            dma((4, GROUP)),
+            dma((4, GROUP)),
             dma((PAIR, GROUP)),
             dma((PAIR, GROUP)),
             dma((PAIR, 8)),
@@ -606,10 +635,9 @@
             dma((PLANE,)),
             dma((PLANE,)),
             dma(()),
-            dma(()),
         ],
         compiler_params=pltpu.CompilerParams(
-            collective_id=1, has_side_effects=True, vmem_limit_bytes=48 * 1024 * 1024
+            collective_id=1, has_side_effects=True, vmem_limit_bytes=VMEM_LIMIT
         ),
         name="sweeps",
     )(probes, slow, absorb, partition)

time: 91.1 us -> 67.7 us (0.74)
  Pallas kernels: 85.2 us -> 64 us
  local copies, waits for them, and re-layouts: 5.06 us -> 2.93 us
    pallas_call x1, Pallas kernels: 85.2 us -> 64 us  [swept(): pl.pallas_call(kernel, out_shape=(jax.ShapeDtypeStruct((2 * PROBES * 64,...]
    unnamed x10 -> x4, local copies, waits for them, and re-layouts: 5.06 us -> 2.93 us
where the time goes in v2:
time: 67.7 us; the launch traced here: 67.6 us
  Pallas kernels  64 us (95%)
  local copies, waits for them, and re-layouts  2.93 us (4%)
    pallas_call x1, Pallas kernels, swept(): pl.pallas_call(kernel, out_shape=(jax.ShapeDtypeStruct((2 * PROBES * 64,...  64 us
    unnamed x4, local copies, waits for them, and re-layouts  2.93 us

profile of v2, /device:TPU:1, one launch (start us, length us, event | category | flops | bytes accessed | tf_op | source)
XLA Modules:
  0.0 67.6 jit_solution(7846599738826726766)
XLA Ops:
  0.6 64.0 %sweeps.1 = (f32[2048,128]{1,0:T(8,128)}, f32[2,32,64]{2,1,0:T(8,128)}) custom-call(f32[2048,128]{1,0:T(8,128)} %bitcast.17, f32[64,128]{1,0:T(8,128)} %bitcast.20, s32[2]{0:T(128)} %absorb.1, s32[128,128]{1,0:T(8,128)} %bitcast.19), custom_call_target="tpu_custom_call" | custom-call | tf_op jit(solution)/shard_map/sweeps/pallas_call | solution.py:591
  64.6 0.0 copy-start
  64.6 2.3 %copy.11 = f32[16,2,2,4096]{3,2,1,0:T(2,128)} copy(f32[16,2,2,4096]{3,2,1,0:T(2,128)} %bitcast.18) | data formatting | bytes 2097152
  66.9 0.0 copy-done
  67.0 0.6 copy.12
Async XLA Ops:
  64.6 2.3 %copy-start = (f32[2,32,64]{2,1,0:T(8,128)S(1)}, f32[2,32,64]{2,1,0:T(8,128)}, u32[]{:S(2)}) copy-start(f32[2,32,64]{2,1,0:T(8,128)} %get-tuple-element.5) | copy-start | bytes 49156

commit v3 on v2

v3 whole, which is shorter than its diff:
```python
import functools

import jax
import jax.numpy as jnp
from jax import lax
from jax.experimental import pallas as pl
from jax.experimental.pallas import tpu as pltpu
from jax.sharding import PartitionSpec as P

ITERS = 9
BS = 64
SHIFTS = ((0, 0), (1, 0), (3, 0), (0, 1), (2, 0), (1, 1), (3, 1), (2, 1))
TAKE = (2, 2, 2, 2, 0, 0, 0, 0, 0, 0)
LAST = 1
WINDOW = 16
BLOCK = 8
OMEGA = 0.8
BETA = 0.5
SIGMA = 1.5

MESH = pl.DeviceIdType.MESH
PLANE = 32
GROUP = 8
PROBES = 16
PAIR = 2
OWN = 2 * GROUP
HALO = 8
ROWS = OWN + 2 * HALO
MAIN = 4
WIDE = 6
POS = 64
F32 = jnp.float32
VMEM_LIMIT = 62 * 1024 * 1024


def lanes():
    return lax.broadcasted_iota(jnp.int32, (8, 128), 1)


def sublanes():
    return lax.broadcasted_iota(jnp.int32, (8, 128), 0)


def widen(tiles, left, right, left_at, right_at):
    lane = lanes()
    first, last = tiles[0], tiles[3]
    before = jnp.where(lane < 32, pltpu.roll(last, 33, 1), pltpu.roll(last, 32, 1))
    before = jnp.where(lane == 0, pltpu.roll(left, (128 - left_at) % 128, 1), before)
    after = jnp.where(lane < 96, pltpu.roll(first, 96, 1), pltpu.roll(first, 95, 1))
    after = jnp.where(lane == 127, pltpu.roll(right, (255 - right_at) % 128, 1), after)
    return [before] + list(tiles) + [after]


def swap_blocks(v):
    lane = lanes()
    low, even = lane < 64, (lane & 32) == 0
    a = [None] * 4
    for h in range(2):
        a[h] = jnp.where(low, v[h], pltpu.roll(v[h + 2], 64, 1))
        a[h + 2] = jnp.where(low, pltpu.roll(v[h], 64, 1), v[h + 2])
    out = [None] * 4
    for h in (0, 2):
        out[h] = jnp.where(even, a[h], pltpu.roll(a[h + 1], 32, 1))
        out[h + 1] = jnp.where(even, pltpu.roll(a[h], 96, 1), a[h + 1])
    return out


def to_lanes(chunks):
    turned = jnp.concatenate(chunks, axis=0).T
    by_tile = [swap_blocks([turned[32 * h + 8 * j : 32 * h + 8 * j + 8] for h in range(4)]) for j in range(MAIN)]
    return [[by_tile[j][n] for j in range(MAIN)] for n in range(4)]


def to_chunks(rows):
    by_tile = [swap_blocks([rows[n][j] for n in range(4)]) for j in range(MAIN)]
    return jnp.concatenate([by_tile[j][h] for h in range(4) for j in range(MAIN)], axis=0).T


def kernel(
    probes, slow, absorb, partition,
    field, bases,
    inbuf, slowbuf, flags, esend, erecv, sendf, ssend, epack, fbuf, sbuf, ebuf, coef, gbuf, ubuf, vbuf, obuf, rbuf,
    points, tsend, tbuf, picked, gat, mats,
    in_sem, es, er, own_sem, fs, fr, zs, zr, rs, rr,
    ts, tr, town, gs, gr, gown,
):
    layer = lax.axis_index("layer")
    strip = lax.axis_index("strip")
    z = layer // GROUP
    me = lax.rem(layer, GROUP)

    mine_x, mine_y = lax.rem(me, 4), me // 4

    def peer_of(j):
        dx, dy = SHIFTS[j]
        return lax.rem(mine_y + dy, 2) * 4 + lax.rem(mine_x + dx, 4)

    def from_of(j):
        dx, dy = SHIFTS[j]
        return lax.rem(mine_y + dy, 2) * 4 + lax.rem(mine_x + 4 - dx, 4)

    def member(m):
        return (z * GROUP + m, strip)

    place = me * 4 + strip

    def in_plane(d):
        return (z * GROUP + d // 4, lax.rem(d, 4))

    up_id = (layer - GROUP, strip)
    down_id = (layer + GROUP, strip)

    copies = [
        pltpu.make_async_copy(probes, inbuf, in_sem.at[0]),
        pltpu.make_async_copy(slow, slowbuf, in_sem.at[1]),
        pltpu.make_async_copy(absorb, flags, in_sem.at[2]),
        pltpu.make_async_copy(partition.at[pl.ds(16 * z, 16)], points, in_sem.at[3]),
    ]
    for c in copies:
        c.start()

    barrier = pltpu.get_barrier_semaphore()
    for j in range(1, PLANE):
        pl.semaphore_signal(barrier, inc=1, device_id=in_plane(lax.rem(place + j, PLANE)), device_id_type=MESH)

    def meets(other):
        return (z == 3) | (z == 4) | (other == 3) | (other == 4) | (other == z + 1) | (other == z - 1)

    greeted = PLANE - 1
    for dz in range(1, 8):
        other = lax.rem(z + dz, 8)
        greeted = greeted + jnp.where(meets(other), 1, 0)

        @pl.when(meets(other))
        def _():
            pl.semaphore_signal(barrier, inc=1, device_id=(other * GROUP + me, strip), device_id_type=MESH)

    @pl.when(strip == 0)
    def _():
        erecv[0] = jnp.zeros_like(erecv[0])

    @pl.when(strip == 3)
    def _():
        erecv[1] = jnp.zeros_like(erecv[1])

    @pl.when(z == 0)
    def _():
        for p in range(PAIR):
            fbuf[p, 0:HALO] = jnp.zeros((HALO, 2, MAIN, 8, 128), F32)
        sbuf[0:HALO] = jnp.zeros((HALO, MAIN, 8, 128), F32)
        ebuf[0:4] = jnp.zeros((4, 4, 8, 128), F32)

    @pl.when(z == 7)
    def _():
        for p in range(PAIR):
            fbuf[p, HALO + OWN : ROWS] = jnp.zeros((HALO, 2, MAIN, 8, 128), F32)
        sbuf[HALO + OWN : ROWS] = jnp.zeros((HALO, MAIN, 8, 128), F32)
        ebuf[12:16] = jnp.zeros((4, 4, 8, 128), F32)

    for c in copies:
        c.wait()

    for side, chunk in ((0, 0), (1, 31)):
        rows = []
        for r in range(2):
            at = 2 * chunk + r
            rows += [inbuf[pl.ds(512 * q + at, 8, stride=64), :] for q in range(4)]
            rows.append(jnp.broadcast_to(slowbuf[at : at + 1, :], (8, 128)))
        rows.append(jnp.zeros((48, 128), F32))
        turned = jnp.concatenate(rows, axis=0).T
        esend[side] = turned[0:8] if side == 0 else turned[120:128]

    def stage_f(p):
        for m in range(GROUP):
            base = (2 * m + p) * 128
            four = to_lanes([inbuf[pl.ds(base + 64 * c + r, 32, stride=2), :] for r in range(2) for c in range(2)])
            for r in range(2):
                for c in range(2):
                    for t in range(MAIN):
                        sendf[p, m, r, c, t] = four[2 * r + c][t]

    def stage_s():
        two = [slowbuf[pl.ds(r, 32, stride=2), :] for r in range(2)]
        four = to_lanes(two + two)
        for r in range(2):
            for t in range(MAIN):
                ssend[r, t] = four[r][t]

    stage_f(0)
    stage_s()
    stage_f(1)
    pl.semaphore_wait(barrier, greeted)

    def edge_copy(side, to):
        return pltpu.make_async_remote_copy(
            src_ref=esend.at[side], dst_ref=erecv.at[1 - side], send_sem=es.at[side], recv_sem=er.at[1 - side],
            device_id=(layer, to), device_id_type=MESH,
        )

    @pl.when(strip > 0)
    def _():
        edge_copy(0, strip - 1).start()

    @pl.when(strip < 3)
    def _():
        edge_copy(1, strip + 1).start()

    def rows_of(m):
        return pl.ds(HALO + 2 * m, 2)

    def f_copy(p, j, dst_member, to):
        return pltpu.make_async_remote_copy(
            src_ref=sendf.at[p, to], dst_ref=fbuf.at[p, rows_of(dst_member)], send_sem=fs.at[p, j], recv_sem=fr.at[p, j],
            device_id=member(to), device_id_type=MESH,
        )

    def s_copy(j, dst_member, to):
        return pltpu.make_async_remote_copy(
            src_ref=ssend, dst_ref=sbuf.at[rows_of(dst_member)], send_sem=fs.at[2, j], recv_sem=fr.at[2, j],
            device_id=member(to), device_id_type=MESH,
        )

    def e_copy(j, dst_member, to):
        return pltpu.make_async_remote_copy(
            src_ref=epack, dst_ref=ebuf.at[4 + dst_member], send_sem=fs.at[3, j], recv_sem=fr.at[3, j],
            device_id=member(to), device_id_type=MESH,
        )

    def own_f(p):
        return pltpu.make_async_copy(sendf.at[p, me], fbuf.at[p, rows_of(me)], own_sem.at[p])

    own_s = pltpu.make_async_copy(ssend, sbuf.at[rows_of(me)], own_sem.at[2])
    own_e = pltpu.make_async_copy(epack, ebuf.at[4 + me], own_sem.at[5])

    def stage_e():
        for side in range(2):
            epack[side] = erecv[side]
        for r in range(2):
            epack[2 + r] = jnp.full((8, 128), flags[r], jnp.int32).astype(F32)

    def launch(k, j):
        if j == 0:
            (own_e if k == 3 else own_s if k == 2 else own_f(k)).start()
        elif k == 3:
            e_copy(j, me, peer_of(j)).start()
        elif k == 2:
            s_copy(j, me, peer_of(j)).start()
        else:
            f_copy(k, j, me, peer_of(j)).start()

    early = [(0, j) for j in range(GROUP)] + [(2, j) for j in range(GROUP)] + [(3, j) for j in range(GROUP)]
    late = [(1, j) for j in range(GROUP)]
    queue = early + late

    ready = min(WINDOW + 1, 2 * GROUP)
    for k, j in queue[:ready]:
        launch(k, j)

    @pl.when(strip > 0)
    def _():
        edge_copy(0, strip - 1).wait_send()
        edge_copy(1, strip - 1).wait_recv()

    @pl.when(strip < 3)
    def _():
        edge_copy(1, strip + 1).wait_send()
        edge_copy(0, strip + 1).wait_recv()

    stage_e()
    for k, j in queue[ready : WINDOW + 1]:
        launch(k, j)

    def forward_ref(k, pair):
        return ebuf.at[pair] if k == 3 else (sbuf if k == 2 else fbuf.at[k]).at[pl.ds(2 * pair, 2)]

    def up_copy(k, j, m):
        return pltpu.make_async_remote_copy(
            src_ref=forward_ref(k, 4 + m), dst_ref=forward_ref(k, 12 + m),
            send_sem=zs.at[k, j], recv_sem=zr.at[k, j], device_id=up_id, device_id_type=MESH,
        )

    def down_copy(k, j, m):
        return pltpu.make_async_remote_copy(
            src_ref=forward_ref(k, 4 + m), dst_ref=forward_ref(k, m - 4),
            send_sem=zs.at[k, j], recv_sem=zr.at[k, j], device_id=down_id, device_id_type=MESH,
        )

    def arrive(k, j):
        m = from_of(j)
        if j == 0:
            (own_e if k == 3 else own_s if k == 2 else own_f(k)).wait()
        elif k == 2:
            s_copy(j, m, peer_of(j)).wait_recv()
        elif k == 3:
            e_copy(j, m, peer_of(j)).wait_recv()
        else:
            f_copy(k, j, m, peer_of(j)).wait_recv()

        @pl.when((m < 4) & (z > 0))
        def _():
            up_copy(k, j, m).start()

        @pl.when((m >= 4) & (z < 7))
        def _():
            down_copy(k, j, m).start()

    def halo_wait(k):
        for j in range(GROUP):
            m = from_of(j)

            @pl.when((m < 4) & (z < 7))
            def _():
                up_copy(k, j, m).wait_recv()

            @pl.when((m >= 4) & (z > 0))
            def _():
                down_copy(k, j, m).wait_recv()

    def advance(i):
        arrive(*queue[i])
        if i + WINDOW + 1 < len(queue):
            launch(*queue[i + WINDOW + 1])

    for i in range(len(early)):
        advance(i)
    halo_wait(2)
    halo_wait(3)

    def by_pairs(work):
        def two(i, carry):
            for n in range(2):
                work(2 * i + n)
            return carry

        lax.fori_loop(0, ROWS // 4, two, 0)

    def coef_pair(pair):
        lane = lanes()
        left, right = ebuf[pair, 0], ebuf[pair, 1]
        inside = ((pair >= 4) | (z > 0)) & ((pair < 12) | (z < 7))
        for n in range(2):
            r = 2 * pair + n
            flag = ebuf[pair, 2 + n]
            wide = widen([sbuf[r, t] for t in range(MAIN)], left, right, 40 * n + 32, 40 * n + 32)
            for t in range(WIDE):
                dre = 4.0 - wide[t]
                dim = BETA * wide[t] + SIGMA * flag
                scale = OMEGA / (dre * dre + dim * dim)
                keep = jnp.full((8, 128), inside)
                if t == 0:
                    keep = keep & ((lane > 0) | jnp.full((8, 128), strip > 0))
                if t == WIDE - 1:
                    keep = keep & ((lane < 127) | jnp.full((8, 128), strip < 3))
                coef[r, 0, 8 + 8 * t : 16 + 8 * t] = jnp.where(keep, dre * scale, 0.0)
                coef[r, 1, 8 + 8 * t : 16 + 8 * t] = jnp.where(keep, -dim * scale, 0.0)

    by_pairs(coef_pair)
    halo_wait(0)

    def source_row(p):
        def pair_of(pair):
            left = pltpu.roll(ebuf[pair, 0], lax.rem(128 - 4 * me, 128), 1)
            right = pltpu.roll(ebuf[pair, 1], lax.rem(128 - 4 * me, 128), 1)
            for n in range(2):
                r = 2 * pair + n
                wide = []
                for c in range(2):
                    at = 40 * n + 2 * p + c
                    wide.append(widen([fbuf[p, r, c, t] for t in range(MAIN)], left, right, at, at))
                for t in range(WIDE):
                    at = slice(8 + 8 * t, 16 + 8 * t)
                    er_, ei_ = coef[r, 0, at], coef[r, 1, at]
                    fr_, fi_ = wide[0][t], wide[1][t]
                    gbuf[p, r, 0, at] = er_ * fr_ - ei_ * fi_
                    gbuf[p, r, 1, at] = er_ * fi_ + ei_ * fr_

        by_pairs(pair_of)

    def sweep(p, step, middle=None):
        src = gbuf if step == 2 else (ubuf if step % 2 else vbuf)
        dst = vbuf if step % 2 else ubuf
        start, tiles = (8, 6) if step < 5 else (12, 5) if step < ITERS else (16, 4)
        if middle is None:
            low, count = step - 1, ROWS + 2 - 2 * step
            block = {30: 5, 28: 4, 26: 2, 24: 4, 22: 2, 20: 4, 18: 3, 16: 4}[count]
        else:
            low, count = middle - (ITERS - step), 2 * (ITERS - step) + 1
            block = {15: 5, 13: 1, 11: 1, 9: 3, 7: 1, 5: 5, 3: 3, 1: 1}[count]
        spans = [slice(start + 8 * t, start + 8 * t + 8) for t in range(tiles)]

        def load(r):
            return [src[p, r, c, at] for c in range(2) for at in spans]

        def body(i, carry):
            above, here = list(carry[: 2 * tiles]), list(carry[2 * tiles :])
            for n in range(block):
                r = low + block * i + n
                below = load(r + 1)
                near = [
                    src[p, r, c, at.start - 1 : at.stop - 1] + src[p, r, c, at.start + 1 : at.stop + 1]
                    for c in range(2)
                    for at in spans
                ]
                for t, at in enumerate(spans):
                    er_, ei_ = coef[r, 0, at], coef[r, 1, at]
                    nr = above[t] + below[t] + near[t]
                    ni = above[tiles + t] + below[tiles + t] + near[tiles + t]
                    new_r = (1.0 - OMEGA) * here[t] + gbuf[p, r, 0, at] + (er_ * nr - ei_ * ni)
                    new_i = (1.0 - OMEGA) * here[tiles + t] + gbuf[p, r, 1, at] + (er_ * ni + ei_ * nr)
                    if step < ITERS:
                        dst[p, r, 0, at], dst[p, r, 1, at] = new_r, new_i
                    elif middle is None:
                        obuf[p, r - HALO, 0, t], obuf[p, r - HALO, 1, t] = new_r, new_i
                    else:
                        tsend[0, t], tsend[1, t] = new_r, new_i
                above, here = here, below
            return tuple(above) + tuple(here)

        lax.fori_loop(0, count // block, body, tuple(load(low - 1)) + tuple(load(low)))

    def back_copy(p, j, of_member, to):
        return pltpu.make_async_remote_copy(
            src_ref=obuf.at[p, pl.ds(2 * to, 2)], dst_ref=rbuf.at[2 * of_member + p], send_sem=rs.at[p, j], recv_sem=rr.at[p, j],
            device_id=member(to), device_id_type=MESH,
        )

    def own_back(p):
        return pltpu.make_async_copy(obuf.at[p, pl.ds(2 * me, 2)], rbuf.at[2 * me + p], own_sem.at[3 + p])

    def send_back(p):
        for j in range(1, GROUP):
            back_copy(p, j, me, peer_of(j)).start()
        own_back(p).start()

    def receive_back(p):
        for first in (0, 4):
            for j in range(first, first + 4):
                if j == 0:
                    own_back(p).wait()
                else:
                    back_copy(p, j, from_of(j), peer_of(j)).wait_recv()
            for j in range(first, first + 4):
                q = 2 * from_of(j) + p
                rows = to_chunks([[rbuf[q, r, c, t] for t in range(MAIN)] for r in range(2) for c in range(2)])
                for r in range(2):
                    for c in range(2):
                        n = 2 * r + c
                        field[pl.ds(q * 128 + 64 * c + r, 32, stride=2), :] = rows[32 * n : 32 * n + 32]

    def trace_row(side, p):
        return tsend if p else obuf.at[p, OWN - 1 if side == 0 else 0]

    def trace_copy(side, p, other):
        return pltpu.make_async_remote_copy(
            src_ref=trace_row(side, p), dst_ref=tbuf.at[side, p],
            send_sem=ts.at[p, other], recv_sem=tr.at[side, p],
            device_id=(other * GROUP + me, strip), device_id_type=MESH,
        )

    def trace_own(side, p):
        return pltpu.make_async_copy(trace_row(side, p), tbuf.at[side, p], town.at[p])

    def trace_send(p):
        for side in range(2):
            owner = 3 + side

            @pl.when(z == owner)
            def _():
                for other in range(8):
                    if other == owner:
                        trace_own(side, p).start()
                    else:
                        trace_copy(side, p, other).start()

    def trace_wait(p):
        for side in range(2):
            owner = 3 + side

            @pl.when(z == owner)
            def _():
                trace_own(side, p).wait()

            @pl.when(z != owner)
            def _():
                trace_copy(side, p, 0).wait_recv()

    def pick(p, g):
        sub = sublanes()
        at = jnp.broadcast_to(points[pl.ds(g, 1), :], (8, 128)) - strip * 4096
        tile, lane = (at >> 3) & 3, (at & 96) | ((at >> 7) & 31)
        hit = ((at >> 12) == 0) & ((at & 7) == sub)
        rows = jnp.zeros((8, 128), F32) if p == 0 else picked[g]
        for side in range(2):
            for c in range(2):
                got = [jnp.take_along_axis(tbuf[side, p, c, t], lane, axis=1) for t in range(MAIN)]
                best = got[0]
                for t in range(1, MAIN):
                    best = jnp.where(tile == t, got[t], best)
                one = jnp.sum(jnp.where(hit, best, 0.0), axis=0, keepdims=True)
                rows = jnp.where(sub == side * 4 + p * 2 + c, jnp.broadcast_to(one, (8, 128)), rows)
        picked[g] = rows

    def pick_all(p):
        def four(i, carry):
            for n in range(4):
                pick(p, 4 * i + n)
            return carry

        lax.fori_loop(0, 4, four, 0)

    def picked_copy(j, source, to):
        return pltpu.make_async_remote_copy(
            src_ref=picked.at[to // 2], dst_ref=gat.at[source], send_sem=gs.at[j], recv_sem=gr.at[j],
            device_id=in_plane(to), device_id_type=MESH,
        )

    picked_own = pltpu.make_async_copy(picked.at[place // 2], gat.at[place], gown)

    def pick_send():
        pick_all(1)
        for j in range(1, PLANE):
            picked_copy(j, place, lax.rem(place + j, PLANE)).start()
        picked_own.start()

    def compress():
        for j in range(1, PLANE):
            picked_copy(j, lax.rem(place + PLANE - j, PLANE), lax.rem(place + j, PLANE)).wait_recv()
        picked_own.wait()
        lane32 = lax.broadcasted_iota(jnp.int32, (32, 128), 1)
        row32 = lax.broadcasted_iota(jnp.int32, (32, 128), 0)
        odd = jnp.full((8, 128), lax.rem(strip, 2) == 1)
        for m in range(GROUP):
            tile = (gat[4 * m] + gat[4 * m + 1]) + (gat[4 * m + 2] + gat[4 * m + 3])
            tile = jnp.where(odd, pltpu.roll(tile, 64, 1), tile)
            tile = jnp.where(lanes() < 64, tile, 0.0)
            for side in range(2):
                mats[side, 4 * m : 4 * m + 4, :] = tile[4 * side : 4 * side + 4, :]
        augmented = []
        for side in range(2):
            mat = mats[side]
            zero = jnp.zeros((32, 128), F32)
            spread = jnp.concatenate([zero, zero, mat, zero], axis=0)
            gram = lax.dot_general(
                mat, spread, (((1,), (1,)), ((), ())), precision=lax.Precision.HIGHEST, preferred_element_type=F32
            )
            augmented.append(jnp.where(lane32 < 64, mat, gram))
        for first in range(0, 32, BLOCK):
            spread = [
                [jnp.broadcast_to(a[:, 64 + k : 65 + k], (32, 128)) for k in range(first, first + BLOCK)] for a in augmented
            ]
            for j in range(BLOCK):
                k = first + j
                for side in range(2):
                    a, columns = augmented[side], spread[side]
                    inverse = lax.rsqrt(jnp.broadcast_to(columns[j][k : k + 1, :], (32, 128)))
                    row = jnp.broadcast_to(a[k : k + 1, :], (32, 128)) * inverse
                    column = columns[j] * inverse
                    augmented[side] = jnp.where(row32 > k, a - column * row, jnp.where(row32 == k, row, a))
                    for i in range(j + 1, BLOCK):
                        across = jnp.broadcast_to(columns[i][k : k + 1, :], (32, 128)) * inverse
                        columns[i] = columns[i] - column * across
        for side in range(2):
            bases[side] = augmented[side][:, :BS]

    later = iter(range(len(early), len(queue)))

    def take(n):
        for _ in range(n):
            advance(next(later))

    take(TAKE[0])
    source_row(0)
    take(TAKE[1])
    for step in range(2, ITERS + 1):
        sweep(0, step)
        take(TAKE[step])
    trace_send(0)
    send_back(0)
    halo_wait(1)
    source_row(1)

    @pl.when((z == 3) | (z == 4))
    def _():
        for step in range(2, ITERS + 1):
            sweep(1, step, jnp.where(z == 3, HALO + OWN - 1, HALO))
        trace_send(1)

    for step in range(2, ITERS + 1):
        sweep(1, step)
    send_back(1)
    trace_wait(0)
    pick_all(0)
    receive_back(0)
    trace_wait(1)
    pick_send()
    if LAST == 0:
        compress()
    receive_back(1)
    if LAST == 1:
        compress()

    for j in range(1, GROUP):
        for p in range(PAIR):
            f_copy(p, j, me, peer_of(j)).wait_send()
            back_copy(p, j, me, peer_of(j)).wait_send()
        s_copy(j, me, peer_of(j)).wait_send()
        e_copy(j, me, peer_of(j)).wait_send()
    for k in range(4):
        for j in range(GROUP):
            m = from_of(j)

            @pl.when((m < 4) & (z > 0))
            def _():
                up_copy(k, j, m).wait_send()

            @pl.when((m >= 4) & (z < 7))
            def _():
                down_copy(k, j, m).wait_send()

    for p in range(PAIR):
        for side in range(2):

            @pl.when(z == 3 + side)
            def _():
                for other in range(8):
                    if other != 3 + side:
                        trace_copy(side, p, other).wait_send()

    for j in range(1, PLANE):
        picked_copy(j, place, lax.rem(place + j, PLANE)).wait_send()


def swept(probes, slow, absorb, partition):
    far = pl.BlockSpec(memory_space=pltpu.HBM)
    near = pl.BlockSpec(memory_space=pltpu.VMEM)
    dma = pltpu.SemaphoreType.DMA
    return pl.pallas_call(
        kernel,
        out_shape=(
            jax.ShapeDtypeStruct((2 * PROBES * 64, 128), F32),
            jax.ShapeDtypeStruct((2, 2 * PROBES, BS), F32),
        ),
        in_specs=[far] * 4,
        out_specs=(near, near),
        scratch_shapes=[
            pltpu.VMEM((2 * PROBES * 64, 128), F32),
            pltpu.VMEM((64, 128), F32),
            pltpu.SMEM((2,), jnp.int32),
            pltpu.VMEM((2, 8, 128), F32),
            pltpu.VMEM((2, 8, 128), F32),
            pltpu.VMEM((PAIR, GROUP, 2, 2, MAIN, 8, 128), F32),
            pltpu.VMEM((2, MAIN, 8, 128), F32),
            pltpu.VMEM((4, 8, 128), F32),
            pltpu.VMEM((PAIR, ROWS, 2, MAIN, 8, 128), F32),
            pltpu.VMEM((ROWS, MAIN, 8, 128), F32),
            pltpu.VMEM((ROWS // 2, 4, 8, 128), F32),
            pltpu.VMEM((ROWS, 2, POS, 128), F32),
            pltpu.VMEM((PAIR, ROWS, 2, POS, 128), F32),
            pltpu.VMEM((PAIR, ROWS, 2, POS, 128), F32),
            pltpu.VMEM((PAIR, ROWS, 2, POS, 128), F32),
            pltpu.VMEM((PAIR, OWN, 2, MAIN, 8, 128), F32),
            pltpu.VMEM((PROBES, 2, 2, MAIN, 8, 128), F32),
            pltpu.VMEM((16, 128), jnp.int32),
            pltpu.VMEM((2, MAIN, 8, 128), F32),
            pltpu.VMEM((2, PAIR, 2, MAIN, 8, 128), F32),
            pltpu.VMEM((16, 8, 128), F32),
            pltpu.VMEM((PLANE, 8, 128), F32),
            pltpu.VMEM((2, 32, 128), F32),
            dma((4,)),
            dma((2,)),
            dma((2,)),
            dma((6,)),
            dma((4, GROUP)),
            dma((4, GROUP)),
            dma((4, GROUP)),
            dma((4, GROUP)),
            dma((PAIR, GROUP)),
            dma((PAIR, GROUP)),
            dma((PAIR, 8)),
            dma((2, PAIR)),
            dma((PAIR,)),
            dma((PLANE,)),
            dma((PLANE,)),
            dma(()),
        ],
        compiler_params=pltpu.CompilerParams(
            collective_id=1, has_side_effects=True, vmem_limit_bytes=VMEM_LIMIT
        ),
        name="sweeps",
    )(probes, slow, absorb, partition)


def per_device(probes, slowness, absorbing, partition):
    flat = probes.reshape(PROBES, 2, 2, 32, 128).transpose(0, 1, 3, 2, 4).reshape(2 * PROBES * 64, 128)
    slow = slowness.reshape(2, 32, 128).transpose(1, 0, 2).reshape(64, 128)
    out, bases = swept(flat, slow, absorbing, partition.reshape(128, 128))
    field = out.reshape(PROBES, 2, 32, 2, 128).transpose(0, 1, 3, 2, 4).reshape(PROBES, 2, 2, 4096)
    return field, bases[None]


def solution(mesh):
    return jax.shard_map(
        per_device,
        mesh=mesh,
        in_specs=(P(None, None, "layer", "strip"), P("layer", "strip"), P("layer"), P()),
        out_specs=(P(None, None, "layer", "strip"), P(("layer", "strip"), None, None, None)),
        check_vma=False,
    )
```

time: 67.7 us -> 60.6 us (0.90)
  Pallas kernels: 64 us -> 56.9 us
    pallas_call x1, Pallas kernels: 64 us -> 56.9 us  [swept(): pl.pallas_call(kernel, out_shape=(jax.ShapeDtypeStruct((2 * PROBES * 64,...]
where the time goes in v3:
time: 60.6 us; the launch traced here: 60.4 us
  Pallas kernels  56.9 us (94%)
  local copies, waits for them, and re-layouts  2.93 us (5%)
  between operations  0.65 us (1%)
    pallas_call x1, Pallas kernels, swept(): pl.pallas_call(kernel, out_shape=(jax.ShapeDtypeStruct((2 * PROBES * 64,...  56.9 us
    unnamed x4, local copies, waits for them, and re-layouts  2.93 us

profile of v3, /device:TPU:1, one launch (start us, length us, event | category | flops | bytes accessed | tf_op | source)
XLA Modules:
  0.0 60.4 jit_solution(13789784061295318118)
XLA Ops:
  0.6 56.9 %sweeps.1 = (f32[2048,128]{1,0:T(8,128)}, f32[2,32,64]{2,1,0:T(8,128)}) custom-call(f32[2048,128]{1,0:T(8,128)} %bitcast.17, f32[64,128]{1,0:T(8,128)} %bitcast.20, s32[2]{0:T(128)} %absorb.1, s32[128,128]{1,0:T(8,128)} %bitcast.19), custom_call_target="tpu_custom_call" | custom-call | tf_op jit(solution)/shard_map/sweeps/pallas_call | solution.py:637
  57.5 0.0 copy-start
  57.5 2.3 %copy.11 = f32[16,2,2,4096]{3,2,1,0:T(2,128)} copy(f32[16,2,2,4096]{3,2,1,0:T(2,128)} %bitcast.18) | data formatting | bytes 2097152
  59.8 0.0 copy-done
  59.8 0.6 %copy.12 = f32[1,2,32,64]{3,2,1,0:T(8,128)} copy(f32[1,2,32,64]{3,2,1,0:T(8,128)S(1)} %bitcast.21) | data formatting | bytes 32768
Async XLA Ops:
  57.5 2.3 %copy-start = (f32[2,32,64]{2,1,0:T(8,128)S(1)}, f32[2,32,64]{2,1,0:T(8,128)}, u32[]{:S(2)}) copy-start(f32[2,32,64]{2,1,0:T(8,128)} %get-tuple-element.5) | copy-start | bytes 49156

commit v4 on v3

--- a/solution.py
+++ b/solution.py
@@ -10,9 +10,8 @@
 ITERS = 9
 BS = 64
 SHIFTS = ((0, 0), (1, 0), (3, 0), (0, 1), (2, 0), (1, 1), (3, 1), (2, 1))
-TAKE = (2, 2, 2, 2, 0, 0, 0, 0, 0, 0)
-LAST = 1
-WINDOW = 16
+TAKE = (4, 4, 0, 0, 0, 0, 0, 0, 0, 0)
+WINDOW = 22
 BLOCK = 8
 OMEGA = 0.8
 BETA = 0.5
@@ -590,14 +589,11 @@
     send_back(1)
     trace_wait(0)
     pick_all(0)
-    receive_back(0)
     trace_wait(1)
     pick_send()
-    if LAST == 0:
-        compress()
+    receive_back(0)
     receive_back(1)
-    if LAST == 1:
-        compress()
+    compress()
 
     for j in range(1, GROUP):
         for p in range(PAIR):

time: 60.6 us -> 59.1 us (0.975)
  Pallas kernels: 56.9 us -> 55.4 us
    pallas_call x1, Pallas kernels: 56.9 us -> 55.4 us  [swept(): pl.pallas_call(kernel, out_shape=(jax.ShapeDtypeStruct((2 * PROBES * 64,...]
where the time goes in v4:
time: 59.1 us; the launch traced here: 58.9 us
  Pallas kernels  55.4 us (94%)
  local copies, waits for them, and re-layouts  2.93 us (5%)
  between operations  0.65 us (1%)
    pallas_call x1, Pallas kernels, swept(): pl.pallas_call(kernel, out_shape=(jax.ShapeDtypeStruct((2 * PROBES * 64,...  55.4 us
    unnamed x4, local copies, waits for them, and re-layouts  2.93 us

profile of v4, /device:TPU:1, one launch (start us, length us, event | category | flops | bytes accessed | tf_op | source)
XLA Modules:
  0.0 58.9 jit_solution(5462556821500280867)
XLA Ops:
  0.6 55.4 %sweeps.1 = (f32[2048,128]{1,0:T(8,128)}, f32[2,32,64]{2,1,0:T(8,128)}) custom-call(f32[2048,128]{1,0:T(8,128)} %bitcast.17, f32[64,128]{1,0:T(8,128)} %bitcast.20, s32[2]{0:T(128)} %absorb.1, s32[128,128]{1,0:T(8,128)} %bitcast.19), custom_call_target="tpu_custom_call" | custom-call | tf_op jit(solution)/shard_map/sweeps/pallas_call | solution.py:633
  56.0 0.0 copy-start
  56.0 2.3 %copy.11 = f32[16,2,2,4096]{3,2,1,0:T(2,128)} copy(f32[16,2,2,4096]{3,2,1,0:T(2,128)} %bitcast.18) | data formatting | bytes 2097152
  58.3 0.0 copy-done
  58.3 0.6 %copy.12 = f32[1,2,32,64]{3,2,1,0:T(8,128)} copy(f32[1,2,32,64]{3,2,1,0:T(8,128)S(1)} %bitcast.21) | data formatting | bytes 32768
Async XLA Ops:
  56.0 2.3 %copy-start = (f32[2,32,64]{2,1,0:T(8,128)S(1)}, f32[2,32,64]{2,1,0:T(8,128)}, u32[]{:S(2)}) copy-start(f32[2,32,64]{2,1,0:T(8,128)} %get-tuple-element.5) | copy-start | bytes 49156

commit v5 on v4

--- a/solution.py
+++ b/solution.py
@@ -325,13 +325,13 @@
     halo_wait(2)
     halo_wait(3)
 
-    def by_pairs(work):
+    def by_pairs(work, first=0, count=ROWS // 4):
         def two(i, carry):
             for n in range(2):
-                work(2 * i + n)
+                work(2 * (first + i) + n)
             return carry
 
-        lax.fori_loop(0, ROWS // 4, two, 0)
+        lax.fori_loop(0, count, two, 0)
 
     def coef_pair(pair):
         lane = lanes()
@@ -356,7 +356,7 @@
     by_pairs(coef_pair)
     halo_wait(0)
 
-    def source_row(p):
+    def source_row(p, first=0, count=ROWS // 4):
         def pair_of(pair):
             left = pltpu.roll(ebuf[pair, 0], lax.rem(128 - 4 * me, 128), 1)
             right = pltpu.roll(ebuf[pair, 1], lax.rem(128 - 4 * me, 128), 1)
@@ -373,7 +373,7 @@
                     gbuf[p, r, 0, at] = er_ * fr_ - ei_ * fi_
                     gbuf[p, r, 1, at] = er_ * fi_ + ei_ * fr_
 
-        by_pairs(pair_of)
+        by_pairs(pair_of, first, count)
 
     def sweep(p, step, middle=None):
         src = gbuf if step == 2 else (ubuf if step % 2 else vbuf)
@@ -465,7 +465,7 @@
 
             @pl.when(z == owner)
             def _():
-                for other in range(8):
+                for other in sorted(range(8), key=lambda n: -min((n - owner) % 8, (owner - n) % 8)):
                     if other == owner:
                         trace_own(side, p).start()
                     else:
@@ -576,7 +576,7 @@
     trace_send(0)
     send_back(0)
     halo_wait(1)
-    source_row(1)
+    source_row(1, jnp.where(z == 3, 3, 0), 5)
 
     @pl.when((z == 3) | (z == 4))
     def _():
@@ -584,6 +584,7 @@
             sweep(1, step, jnp.where(z == 3, HALO + OWN - 1, HALO))
         trace_send(1)
 
+    source_row(1, jnp.where(z == 3, 0, 5), 3)
     for step in range(2, ITERS + 1):
         sweep(1, step)
     send_back(1)

time: 59.1 us -> 59.6 us (level)
  no operation moved by 1% of the time
where the time goes in v5:
time: 59.6 us; the launch traced here: 59.5 us
  Pallas kernels  55.9 us (94%)
  local copies, waits for them, and re-layouts  2.93 us (5%)
  between operations  0.65 us (1%)
    pallas_call x1, Pallas kernels, swept(): pl.pallas_call(kernel, out_shape=(jax.ShapeDtypeStruct((2 * PROBES * 64,...  55.9 us
    unnamed x4, local copies, waits for them, and re-layouts  2.93 us

profile of v5, /device:TPU:1, one launch (start us, length us, event | category | flops | bytes accessed | tf_op | source)
XLA Modules:
  0.0 59.5 jit_solution(1755646098566501548)
XLA Ops:
  0.6 55.9 %sweeps.1 = (f32[2048,128]{1,0:T(8,128)}, f32[2,32,64]{2,1,0:T(8,128)}) custom-call(f32[2048,128]{1,0:T(8,128)} %bitcast.17, f32[64,128]{1,0:T(8,128)} %bitcast.20, s32[2]{0:T(128)} %absorb.1, s32[128,128]{1,0:T(8,128)} %bitcast.19), custom_call_target="tpu_custom_call" | custom-call | tf_op jit(solution)/shard_map/sweeps/pallas_call | solution.py:634
  56.5 0.0 copy-start
  56.5 2.3 %copy.11 = f32[16,2,2,4096]{3,2,1,0:T(2,128)} copy(f32[16,2,2,4096]{3,2,1,0:T(2,128)} %bitcast.18) | data formatting | bytes 2097152
  58.8 0.0 copy-done
  58.8 0.6 %copy.12 = f32[1,2,32,64]{3,2,1,0:T(8,128)} copy(f32[1,2,32,64]{3,2,1,0:T(8,128)S(1)} %bitcast.21) | data formatting | bytes 32768
Async XLA Ops:
  56.5 2.3 %copy-start = (f32[2,32,64]{2,1,0:T(8,128)S(1)}, f32[2,32,64]{2,1,0:T(8,128)}, u32[]{:S(2)}) copy-start(f32[2,32,64]{2,1,0:T(8,128)} %get-tuple-element.5) | copy-start | bytes 49156
